TPU v7x, 256 devices: a whole 4x4x8 slice. The times are simulated.
256 devices in a mesh: dx: 16 (over y, x), dy: 16 (over z, core).
Axes of the slice: x: 4, y: 4, z: 8, core: 2. Of those that a mesh axis runs over, the one named last changes fastest.
Arguments:
- volume_fraction: float32 [512, 512, 128], P('dx', 'dy'), may hold values from 0 to 1
- vorticity: float32 [512, 512, 128], P('dx', 'dy'), may hold values from 0.05 to 20
Outputs:
- volume_coeffs: float32 [512, 512, 128], P('dx', 'dy')
- vorticity_coeffs: float32 [512, 512, 128], P('dx', 'dy')
All inputs are finite; a program needn't handle non-finite values.
Results may differ from a plain program's by a relative error of at most 0.00012.
Values sent between devices are 32-bit elements; how exact they have to be, the bound alone decides.
A program may use at most 64 MiB of HBM per device.

v0:
```python
import jax
import jax.numpy as jnp
from jax import lax
from jax.sharding import PartitionSpec as P

LEVELS = 3


LIFT_ALPHA = -1.586134342
LIFT_BETA = -0.05298011854
LIFT_GAMMA = 0.8829110762
LIFT_DELTA = 0.4435068522
LIFT_KAPPA = 1.149604398


def passed_along(value, axis, steps):
    count = lax.axis_size(axis)
    pairs = [(source, (source + steps) % count) for source in range(count)]
    return lax.ppermute(value, axis, pairs)


def lift_core(even_part, odd_part, next_fn, prev_fn):
    odd_part = odd_part + LIFT_ALPHA * (even_part + next_fn(even_part))
    even_part = even_part + LIFT_BETA * (prev_fn(odd_part) + odd_part)
    odd_part = odd_part + LIFT_GAMMA * (even_part + next_fn(even_part))
    even_part = even_part + LIFT_DELTA * (prev_fn(odd_part) + odd_part)
    return (even_part / LIFT_KAPPA, odd_part * LIFT_KAPPA)


def order_matrix(count):
    rows = lax.broadcasted_iota(jnp.int32, (count, count), 0)
    cols = lax.broadcasted_iota(jnp.int32, (count, count), 1)
    target = jnp.where(rows % 2 == 0, rows // 2, count // 2 + rows // 2)
    return (cols == target).astype(jnp.float32)


def apply_last(field, matrix):
    shape = field.shape
    flat = field.reshape(-1, shape[-1])
    moved = jnp.dot(
        flat, matrix, precision=lax.Precision.HIGHEST, preferred_element_type=jnp.float32
    )
    return moved.reshape(shape)


def split_axis(field, along):
    count = field.shape[along]
    paired = field.reshape(field.shape[:along] + (count // 2, 2) + field.shape[along + 1 :])
    return (
        lax.index_in_dim(paired, 0, along + 1, False),
        lax.index_in_dim(paired, 1, along + 1, False),
    )


def alternate(field, along):
    count = field.shape[along]
    low = lax.slice_in_dim(field, 0, count // 2, axis=along)
    high = lax.slice_in_dim(field, count // 2, count, axis=along)
    return jnp.stack([low, high], along + 1).reshape(field.shape)


def edge_fns(along, pairs):

    def next_fn(values):
        return jnp.concatenate(
            [
                lax.slice_in_dim(values, 1, pairs, axis=along),
                lax.slice_in_dim(values, pairs - 1, pairs, axis=along),
            ],
            along,
        )

    def prev_fn(values):
        return jnp.concatenate(
            [
                lax.slice_in_dim(values, 0, 1, axis=along),
                lax.slice_in_dim(values, 0, pairs - 1, axis=along),
            ],
            along,
        )

    return (next_fn, prev_fn)


def lift_depth(field):
    count = field.shape[3]
    half = count // 2
    sorted_field = apply_last(field, order_matrix(count))
    even_part = sorted_field[..., :half]
    odd_part = sorted_field[..., half:]
    next_fn, prev_fn = edge_fns(3, half)
    low, high = lift_core(even_part, odd_part, next_fn, prev_fn)
    return jnp.concatenate([low, high], 3)


def lift_steps(field, along, axis_name):
    even_part, odd_part = split_axis(field, along)
    pairs = even_part.shape[along]

    def next_fn(values):
        first = lax.slice_in_dim(values, 0, 1, axis=along)
        if axis_name == "dx":
            arrived = passed_along(first, "dx", -1)
        else:
            arrived = passed_along(first, "dy", -1)
        return jnp.concatenate([lax.slice_in_dim(values, 1, pairs, axis=along), arrived], along)

    def prev_fn(values):
        last = lax.slice_in_dim(values, pairs - 1, pairs, axis=along)
        if axis_name == "dx":
            arrived = passed_along(last, "dx", 1)
        else:
            arrived = passed_along(last, "dy", 1)
        return jnp.concatenate([arrived, lax.slice_in_dim(values, 0, pairs - 1, axis=along)], along)

    low, high = lift_core(even_part, odd_part, next_fn, prev_fn)
    return jnp.concatenate([low, high], along)


def lift_sharded(field):
    field = lift_steps(field, 1, "dx")
    return lift_steps(field, 2, "dy")


def one_level(field):
    field = lift_depth(field)
    field = lift_sharded(field)
    return field


def transform(field, level):
    sorted_result = one_level(field)
    shape = sorted_result.shape
    if level + 1 < LEVELS:
        corner = sorted_result[:, : shape[1] // 2, : shape[2] // 2, : shape[3] // 2]
        inner = transform(corner, level + 1)
        sorted_result = lax.dynamic_update_slice(sorted_result, inner, (0, 0, 0, 0))
    result = alternate(sorted_result, 1)
    result = alternate(result, 2)
    return apply_last(result, jnp.transpose(order_matrix(shape[3])))


def body(volume_fraction, vorticity):
    stacked = jnp.stack([volume_fraction, vorticity], 0)
    result = transform(stacked, 0)
    return (result[0], result[1])


def solution(mesh):
    placed = (P("dx", "dy", None), P("dx", "dy", None))
    return jax.shard_map(
        body,
        mesh=mesh,
        in_specs=placed,
        out_specs=(P("dx", "dy", None), P("dx", "dy", None)),
        check_vma=False,
    )
```

profile of v0, /device:TPU:0, one launch (start us, length us, event | category | flops | bytes accessed | tf_op | source)
XLA Modules:
  0.0 125.6 jit_solution(16110175114680180197)
XLA Ops:
  0.7 1.9 %fusion = f32[2,32,32,128]{3,2,1,0:T(8,128)S(1)} fusion(f32[1,32,32,128]{3,2,1,0:T(8,128)} %bitcast.201, f32[1,32,32,128]{3,2,1,0:T(8,128)} %bitcast.202, s32[128]{0:T(128)S(1)} %get-tuple-element.49, s32[128]{0:T(128)S(1)} %get-tuple-element.51, s32[128]{0:T(128)S(1)} %get-tuple-element.50, s32[128]{0:T(128)S(1)} %get-tuple-element.52, ...), kind=kOutput, calls=%fused_computation.1 | convolution fusion | flops 403013632 | bytes 2099456 | tf_op jit(solution)/shard_map/dot_general | solution.py:40
  6.7 3.6 %collective-permute-start = (f32[2,1,32,128]{3,1,2,0:T(1,128)S(1)}, f32[2,1,32,128]{3,1,2,0:T(1,128)S(1)}, u32[]{:S(2)}, u32[]{:S(2)}) collective-permute-start(f32[2,1,32,128]{3,1,2,0:T(1,128)S(1)} %slice.445), channel_id=1, source_target_pairs={{0,240},{16,0},{32,16},{48,32},{64,48},{80,64},{96,80},{112,96},{1... | collective-permute-start | bytes 98312 | tf_op jit(solution)/shard_map/ppermute | solution.py:19
  12.7 7.5 %collective-permute-done.1 = f32[2,1,32,128]{3,1,2,0:T(1,128)S(1)} collective-permute-done((f32[2,1,32,128]{3,1,2,0:T(1,128)S(1)}, f32[2,1,32,128]{3,1,2,0:T(1,128)S(1)}, u32[]{:S(2)}, u32[]{:S(2)}) %collective-permute-start.1) | collective-permute-done | bytes 32800 | tf_op jit(solution)/shard_map/ppermute | solution.py:19
  20.6 2.1 %collective-permute-start.2 = (f32[2,1,32,128]{3,1,2,0:T(1,128)S(1)}, f32[2,1,32,128]{3,1,2,0:T(1,128)S(1)}, u32[]{:S(2)}, u32[]{:S(2)}) collective-permute-start(f32[2,1,32,128]{3,1,2,0:T(1,128)S(1)} %slice.449), channel_id=1, source_target_pairs={{0,240},{16,0},{32,16},{48,32},{64,48},{80,64},{96,80},{112,96},{1... | collective-permute-start | bytes 98312 | tf_op jit(solution)/shard_map/ppermute | solution.py:19
  22.8 1.8 %collective-permute-done.2 = f32[2,1,32,128]{3,1,2,0:T(1,128)S(1)} collective-permute-done((f32[2,1,32,128]{3,1,2,0:T(1,128)S(1)}, f32[2,1,32,128]{3,1,2,0:T(1,128)S(1)}, u32[]{:S(2)}, u32[]{:S(2)}) %collective-permute-start.2) | collective-permute-done | bytes 32800 | tf_op jit(solution)/shard_map/ppermute | solution.py:19
  26.6 5.7 %collective-permute-done.3 = f32[2,1,32,128]{3,1,2,0:T(1,128)S(1)} collective-permute-done((f32[2,1,32,128]{3,1,2,0:T(1,128)S(1)}, f32[2,1,32,128]{3,1,2,0:T(1,128)S(1)}, u32[]{:S(2)}, u32[]{:S(2)}) %collective-permute-start.3) | collective-permute-done | bytes 32800 | tf_op jit(solution)/shard_map/ppermute | solution.py:19
  37.0 4.8 %collective-permute-done.5 = f32[2,32,1,128]{3,2,1,0:T(1,128)S(1)} collective-permute-done((f32[2,32,1,128]{3,2,1,0:T(1,128)S(1)}, f32[2,32,1,128]{3,2,1,0:T(1,128)S(1)}, u32[]{:S(2)}, u32[]{:S(2)}) %collective-permute-start.5) | collective-permute-done | bytes 32800 | tf_op jit(solution)/shard_map/ppermute | solution.py:19
  43.8 4.5 %collective-permute-done.7 = f32[2,32,1,128]{3,2,1,0:T(1,128)S(1)} collective-permute-done((f32[2,32,1,128]{3,2,1,0:T(1,128)S(1)}, f32[2,32,1,128]{3,2,1,0:T(1,128)S(1)}, u32[]{:S(2)}, u32[]{:S(2)}) %collective-permute-start.7) | collective-permute-done | bytes 32800 | tf_op jit(solution)/shard_map/ppermute | solution.py:19
  50.3 2.1 %collective-permute-start.8 = (f32[2,1,16,64]{3,1,2,0:T(1,128)S(1)}, f32[2,1,16,64]{3,1,2,0:T(1,128)S(1)}, u32[]{:S(2)}, u32[]{:S(2)}) collective-permute-start(f32[2,1,16,64]{3,1,2,0:T(1,128)S(1)} %slice.476), channel_id=1, source_target_pairs={{0,240},{16,0},{32,16},{48,32},{64,48},{80,64},{96,80},{112,96},{1... | collective-permute-start | bytes 24584 | tf_op jit(solution)/shard_map/ppermute | solution.py:19
  52.4 1.7 %collective-permute-done.8 = f32[2,1,16,64]{3,1,2,0:T(1,128)S(1)} collective-permute-done((f32[2,1,16,64]{3,1,2,0:T(1,128)S(1)}, f32[2,1,16,64]{3,1,2,0:T(1,128)S(1)}, u32[]{:S(2)}, u32[]{:S(2)}) %collective-permute-start.8) | collective-permute-done | bytes 8224 | tf_op jit(solution)/shard_map/ppermute | solution.py:19
  54.3 7.0 %collective-permute-done.9 = f32[2,1,16,64]{3,1,2,0:T(1,128)S(1)} collective-permute-done((f32[2,1,16,64]{3,1,2,0:T(1,128)S(1)}, f32[2,1,16,64]{3,1,2,0:T(1,128)S(1)}, u32[]{:S(2)}, u32[]{:S(2)}) %collective-permute-start.9) | collective-permute-done | bytes 8224 | tf_op jit(solution)/shard_map/ppermute | solution.py:19
  61.5 2.1 %collective-permute-start.10 = (f32[2,1,16,64]{3,1,2,0:T(1,128)S(1)}, f32[2,1,16,64]{3,1,2,0:T(1,128)S(1)}, u32[]{:S(2)}, u32[]{:S(2)}) collective-permute-start(f32[2,1,16,64]{3,1,2,0:T(1,128)S(1)} %slice.480), channel_id=1, source_target_pairs={{0,240},{16,0},{32,16},{48,32},{64,48},{80,64},{96,80},{112,96},{1... | collective-permute-start | bytes 24584 | tf_op jit(solution)/shard_map/ppermute | solution.py:19
  63.6 1.7 %collective-permute-done.10 = f32[2,1,16,64]{3,1,2,0:T(1,128)S(1)} collective-permute-done((f32[2,1,16,64]{3,1,2,0:T(1,128)S(1)}, f32[2,1,16,64]{3,1,2,0:T(1,128)S(1)}, u32[]{:S(2)}, u32[]{:S(2)}) %collective-permute-start.10) | collective-permute-done | bytes 8224 | tf_op jit(solution)/shard_map/ppermute | solution.py:19
  65.7 6.8 %collective-permute-done.11 = f32[2,1,16,64]{3,1,2,0:T(1,128)S(1)} collective-permute-done((f32[2,1,16,64]{3,1,2,0:T(1,128)S(1)}, f32[2,1,16,64]{3,1,2,0:T(1,128)S(1)}, u32[]{:S(2)}, u32[]{:S(2)}) %collective-permute-start.11) | collective-permute-done | bytes 8224 | tf_op jit(solution)/shard_map/ppermute | solution.py:19
  74.3 4.3 %collective-permute-done.13 = f32[2,16,1,64]{3,2,1,0:T(1,128)S(1)} collective-permute-done((f32[2,16,1,64]{3,2,1,0:T(1,128)S(1)}, f32[2,16,1,64]{3,2,1,0:T(1,128)S(1)}, u32[]{:S(2)}, u32[]{:S(2)}) %collective-permute-start.13) | collective-permute-done | bytes 8224 | tf_op jit(solution)/shard_map/ppermute | solution.py:19
  80.3 4.3 %collective-permute-done.15 = f32[2,16,1,64]{3,2,1,0:T(1,128)S(1)} collective-permute-done((f32[2,16,1,64]{3,2,1,0:T(1,128)S(1)}, f32[2,16,1,64]{3,2,1,0:T(1,128)S(1)}, u32[]{:S(2)}, u32[]{:S(2)}) %collective-permute-start.15) | collective-permute-done | bytes 8224 | tf_op jit(solution)/shard_map/ppermute | solution.py:19
  85.9 2.1 %collective-permute-start.16 = (f32[2,1,8,32]{3,2,1,0:T(8,128)S(1)}, f32[2,1,8,32]{3,2,1,0:T(8,128)S(1)}, u32[]{:S(2)}, u32[]{:S(2)}) collective-permute-start(f32[2,1,8,32]{3,2,1,0:T(8,128)S(1)} %slice.507), channel_id=1, source_target_pairs={{0,240},{16,0},{32,16},{48,32},{64,48},{80,64},{96,80},{112,96},{1... | collective-permute-start | bytes 6152 | tf_op jit(solution)/shard_map/ppermute | solution.py:19
  88.0 1.6 %collective-permute-done.16 = f32[2,1,8,32]{3,2,1,0:T(8,128)S(1)} collective-permute-done((f32[2,1,8,32]{3,2,1,0:T(8,128)S(1)}, f32[2,1,8,32]{3,2,1,0:T(8,128)S(1)}, u32[]{:S(2)}, u32[]{:S(2)}) %collective-permute-start.16) | collective-permute-done | bytes 2080 | tf_op jit(solution)/shard_map/ppermute | solution.py:19
  89.7 6.9 %collective-permute-done.17 = f32[2,1,8,32]{3,2,1,0:T(8,128)S(1)} collective-permute-done((f32[2,1,8,32]{3,2,1,0:T(8,128)S(1)}, f32[2,1,8,32]{3,2,1,0:T(8,128)S(1)}, u32[]{:S(2)}, u32[]{:S(2)}) %collective-permute-start.17) | collective-permute-done | bytes 2080 | tf_op jit(solution)/shard_map/ppermute | solution.py:19
  96.7 2.1 %collective-permute-start.18 = (f32[2,1,8,32]{3,2,1,0:T(8,128)S(1)}, f32[2,1,8,32]{3,2,1,0:T(8,128)S(1)}, u32[]{:S(2)}, u32[]{:S(2)}) collective-permute-start(f32[2,1,8,32]{3,2,1,0:T(8,128)S(1)} %slice.511), channel_id=1, source_target_pairs={{0,240},{16,0},{32,16},{48,32},{64,48},{80,64},{96,80},{112,96},{1... | collective-permute-start | bytes 6152 | tf_op jit(solution)/shard_map/ppermute | solution.py:19
  98.8 1.6 %collective-permute-done.18 = f32[2,1,8,32]{3,2,1,0:T(8,128)S(1)} collective-permute-done((f32[2,1,8,32]{3,2,1,0:T(8,128)S(1)}, f32[2,1,8,32]{3,2,1,0:T(8,128)S(1)}, u32[]{:S(2)}, u32[]{:S(2)}) %collective-permute-start.18) | collective-permute-done | bytes 2080 | tf_op jit(solution)/shard_map/ppermute | solution.py:19
  100.8 6.9 %collective-permute-done.19 = f32[2,1,8,32]{3,2,1,0:T(8,128)S(1)} collective-permute-done((f32[2,1,8,32]{3,2,1,0:T(8,128)S(1)}, f32[2,1,8,32]{3,2,1,0:T(8,128)S(1)}, u32[]{:S(2)}, u32[]{:S(2)}) %collective-permute-start.19) | collective-permute-done | bytes 2080 | tf_op jit(solution)/shard_map/ppermute | solution.py:19
  109.4 4.3 %collective-permute-done.21 = f32[2,8,1,32]{3,2,1,0:T(1,128)S(1)} collective-permute-done((f32[2,8,1,32]{3,2,1,0:T(1,128)S(1)}, f32[2,8,1,32]{3,2,1,0:T(1,128)S(1)}, u32[]{:S(2)}, u32[]{:S(2)}) %collective-permute-start.21) | collective-permute-done | bytes 2080 | tf_op jit(solution)/shard_map/ppermute | solution.py:19
  115.2 4.2 %collective-permute-done.23 = f32[2,8,1,32]{3,2,1,0:T(1,128)S(1)} collective-permute-done((f32[2,8,1,32]{3,2,1,0:T(1,128)S(1)}, f32[2,8,1,32]{3,2,1,0:T(1,128)S(1)}, u32[]{:S(2)}, u32[]{:S(2)}) %collective-permute-start.23) | collective-permute-done | bytes 2080 | tf_op jit(solution)/shard_map/ppermute | solution.py:19
  (177 shorter events, 32.0 us)
Async XLA Ops:
  6.7 5.1 %collective-permute-start = (f32[2,1,32,128]{3,1,2,0:T(1,128)S(1)}, f32[2,1,32,128]{3,1,2,0:T(1,128)S(1)}, u32[]{:S(2)}, u32[]{:S(2)}) collective-permute-start(f32[2,1,32,128]{3,1,2,0:T(1,128)S(1)} %slice.445), channel_id=1, source_target_pairs={{0,240},{16,0},{32,16},{48,32},{64,48},{80,64},{96,80},{112,96},{1... | collective-permute-start | bytes 98312 | tf_op jit(solution)/shard_map/ppermute | solution.py:19
  12.6 7.6 %collective-permute-start.1 = (f32[2,1,32,128]{3,1,2,0:T(1,128)S(1)}, f32[2,1,32,128]{3,1,2,0:T(1,128)S(1)}, u32[]{:S(2)}, u32[]{:S(2)}) collective-permute-start(f32[2,1,32,128]{3,1,2,0:T(1,128)S(1)} %slice.446), channel_id=1, source_target_pairs={{0,16},{16,32},{32,48},{48,64},{64,80},{80,96},{96,112},{112,128},... | collective-permute-start | bytes 98312 | tf_op jit(solution)/shard_map/ppermute | solution.py:19
  20.6 4.0 %collective-permute-start.2 = (f32[2,1,32,128]{3,1,2,0:T(1,128)S(1)}, f32[2,1,32,128]{3,1,2,0:T(1,128)S(1)}, u32[]{:S(2)}, u32[]{:S(2)}) collective-permute-start(f32[2,1,32,128]{3,1,2,0:T(1,128)S(1)} %slice.449), channel_id=1, source_target_pairs={{0,240},{16,0},{32,16},{48,32},{64,48},{80,64},{96,80},{112,96},{1... | collective-permute-start | bytes 98312 | tf_op jit(solution)/shard_map/ppermute | solution.py:19
  24.8 7.5 %collective-permute-start.3 = (f32[2,1,32,128]{3,1,2,0:T(1,128)S(1)}, f32[2,1,32,128]{3,1,2,0:T(1,128)S(1)}, u32[]{:S(2)}, u32[]{:S(2)}) collective-permute-start(f32[2,1,32,128]{3,1,2,0:T(1,128)S(1)} %slice.450), channel_id=1, source_target_pairs={{0,16},{16,32},{32,48},{48,64},{64,80},{80,96},{96,112},{112,128},... | collective-permute-start | bytes 98312 | tf_op jit(solution)/shard_map/ppermute | solution.py:19
  33.2 2.6 %collective-permute-start.4 = (f32[2,32,1,128]{3,2,1,0:T(1,128)S(1)}, f32[2,32,1,128]{3,2,1,0:T(1,128)S(1)}, u32[]{:S(2)}, u32[]{:S(2)}) collective-permute-start(f32[2,32,1,128]{3,2,1,0:T(1,128)S(1)} %slice.455), channel_id=1, source_target_pairs={{0,15},{1,0},{2,1},{3,2},{4,3},{5,4},{6,5},{7,6},{8,7},{9,8},{10,9... | collective-permute-start | bytes 98312 | tf_op jit(solution)/shard_map/ppermute | solution.py:19
  35.9 5.9 %collective-permute-start.5 = (f32[2,32,1,128]{3,2,1,0:T(1,128)S(1)}, f32[2,32,1,128]{3,2,1,0:T(1,128)S(1)}, u32[]{:S(2)}, u32[]{:S(2)}) collective-permute-start(f32[2,32,1,128]{3,2,1,0:T(1,128)S(1)} %slice.456), channel_id=1, source_target_pairs={{0,1},{1,2},{2,3},{3,4},{4,5},{5,6},{6,7},{7,8},{8,9},{9,10},{10,1... | collective-permute-start | bytes 98312 | tf_op jit(solution)/shard_map/ppermute | solution.py:19
  41.9 1.6 %collective-permute-start.6 = (f32[2,32,1,128]{3,2,1,0:T(1,128)S(1)}, f32[2,32,1,128]{3,2,1,0:T(1,128)S(1)}, u32[]{:S(2)}, u32[]{:S(2)}) collective-permute-start(f32[2,32,1,128]{3,2,1,0:T(1,128)S(1)} %slice.459), channel_id=1, source_target_pairs={{0,15},{1,0},{2,1},{3,2},{4,3},{5,4},{6,5},{7,6},{8,7},{9,8},{10,9... | collective-permute-start | bytes 98312 | tf_op jit(solution)/shard_map/ppermute | solution.py:19
  43.7 4.6 %collective-permute-start.7 = (f32[2,32,1,128]{3,2,1,0:T(1,128)S(1)}, f32[2,32,1,128]{3,2,1,0:T(1,128)S(1)}, u32[]{:S(2)}, u32[]{:S(2)}) collective-permute-start(f32[2,32,1,128]{3,2,1,0:T(1,128)S(1)} %slice.460), channel_id=1, source_target_pairs={{0,1},{1,2},{2,3},{3,4},{4,5},{5,6},{6,7},{7,8},{8,9},{9,10},{10,1... | collective-permute-start | bytes 98312 | tf_op jit(solution)/shard_map/ppermute | solution.py:19
  50.3 3.8 %collective-permute-start.8 = (f32[2,1,16,64]{3,1,2,0:T(1,128)S(1)}, f32[2,1,16,64]{3,1,2,0:T(1,128)S(1)}, u32[]{:S(2)}, u32[]{:S(2)}) collective-permute-start(f32[2,1,16,64]{3,1,2,0:T(1,128)S(1)} %slice.476), channel_id=1, source_target_pairs={{0,240},{16,0},{32,16},{48,32},{64,48},{80,64},{96,80},{112,96},{1... | collective-permute-start | bytes 24584 | tf_op jit(solution)/shard_map/ppermute | solution.py:19
  54.2 7.1 %collective-permute-start.9 = (f32[2,1,16,64]{3,1,2,0:T(1,128)S(1)}, f32[2,1,16,64]{3,1,2,0:T(1,128)S(1)}, u32[]{:S(2)}, u32[]{:S(2)}) collective-permute-start(f32[2,1,16,64]{3,1,2,0:T(1,128)S(1)} %slice.477), channel_id=1, source_target_pairs={{0,16},{16,32},{32,48},{48,64},{64,80},{80,96},{96,112},{112,128},... | collective-permute-start | bytes 24584 | tf_op jit(solution)/shard_map/ppermute | solution.py:19
  61.5 3.8 %collective-permute-start.10 = (f32[2,1,16,64]{3,1,2,0:T(1,128)S(1)}, f32[2,1,16,64]{3,1,2,0:T(1,128)S(1)}, u32[]{:S(2)}, u32[]{:S(2)}) collective-permute-start(f32[2,1,16,64]{3,1,2,0:T(1,128)S(1)} %slice.480), channel_id=1, source_target_pairs={{0,240},{16,0},{32,16},{48,32},{64,48},{80,64},{96,80},{112,96},{1... | collective-permute-start | bytes 24584 | tf_op jit(solution)/shard_map/ppermute | solution.py:19
  65.4 7.1 %collective-permute-start.11 = (f32[2,1,16,64]{3,1,2,0:T(1,128)S(1)}, f32[2,1,16,64]{3,1,2,0:T(1,128)S(1)}, u32[]{:S(2)}, u32[]{:S(2)}) collective-permute-start(f32[2,1,16,64]{3,1,2,0:T(1,128)S(1)} %slice.481), channel_id=1, source_target_pairs={{0,16},{16,32},{32,48},{48,64},{64,80},{80,96},{96,112},{112,128},... | collective-permute-start | bytes 24584 | tf_op jit(solution)/shard_map/ppermute | solution.py:19
  72.7 1.5 %collective-permute-start.12 = (f32[2,16,1,64]{3,2,1,0:T(1,128)S(1)}, f32[2,16,1,64]{3,2,1,0:T(1,128)S(1)}, u32[]{:S(2)}, u32[]{:S(2)}) collective-permute-start(f32[2,16,1,64]{3,2,1,0:T(1,128)S(1)} %slice.486), channel_id=1, source_target_pairs={{0,15},{1,0},{2,1},{3,2},{4,3},{5,4},{6,5},{7,6},{8,7},{9,8},{10,9... | collective-permute-start | bytes 24584 | tf_op jit(solution)/shard_map/ppermute | solution.py:19
  74.3 4.4 %collective-permute-start.13 = (f32[2,16,1,64]{3,2,1,0:T(1,128)S(1)}, f32[2,16,1,64]{3,2,1,0:T(1,128)S(1)}, u32[]{:S(2)}, u32[]{:S(2)}) collective-permute-start(f32[2,16,1,64]{3,2,1,0:T(1,128)S(1)} %slice.487), channel_id=1, source_target_pairs={{0,1},{1,2},{2,3},{3,4},{4,5},{5,6},{6,7},{7,8},{8,9},{9,10},{10,1... | collective-permute-start | bytes 24584 | tf_op jit(solution)/shard_map/ppermute | solution.py:19
  78.8 1.5 %collective-permute-start.14 = (f32[2,16,1,64]{3,2,1,0:T(1,128)S(1)}, f32[2,16,1,64]{3,2,1,0:T(1,128)S(1)}, u32[]{:S(2)}, u32[]{:S(2)}) collective-permute-start(f32[2,16,1,64]{3,2,1,0:T(1,128)S(1)} %slice.490), channel_id=1, source_target_pairs={{0,15},{1,0},{2,1},{3,2},{4,3},{5,4},{6,5},{7,6},{8,7},{9,8},{10,9... | collective-permute-start | bytes 24584 | tf_op jit(solution)/shard_map/ppermute | solution.py:19
  80.3 4.4 %collective-permute-start.15 = (f32[2,16,1,64]{3,2,1,0:T(1,128)S(1)}, f32[2,16,1,64]{3,2,1,0:T(1,128)S(1)}, u32[]{:S(2)}, u32[]{:S(2)}) collective-permute-start(f32[2,16,1,64]{3,2,1,0:T(1,128)S(1)} %slice.491), channel_id=1, source_target_pairs={{0,1},{1,2},{2,3},{3,4},{4,5},{5,6},{6,7},{7,8},{8,9},{9,10},{10,1... | collective-permute-start | bytes 24584 | tf_op jit(solution)/shard_map/ppermute | solution.py:19
  85.9 3.7 %collective-permute-start.16 = (f32[2,1,8,32]{3,2,1,0:T(8,128)S(1)}, f32[2,1,8,32]{3,2,1,0:T(8,128)S(1)}, u32[]{:S(2)}, u32[]{:S(2)}) collective-permute-start(f32[2,1,8,32]{3,2,1,0:T(8,128)S(1)} %slice.507), channel_id=1, source_target_pairs={{0,240},{16,0},{32,16},{48,32},{64,48},{80,64},{96,80},{112,96},{1... | collective-permute-start | bytes 6152 | tf_op jit(solution)/shard_map/ppermute | solution.py:19
  89.6 7.0 %collective-permute-start.17 = (f32[2,1,8,32]{3,2,1,0:T(8,128)S(1)}, f32[2,1,8,32]{3,2,1,0:T(8,128)S(1)}, u32[]{:S(2)}, u32[]{:S(2)}) collective-permute-start(f32[2,1,8,32]{3,2,1,0:T(8,128)S(1)} %slice.508), channel_id=1, source_target_pairs={{0,16},{16,32},{32,48},{48,64},{64,80},{80,96},{96,112},{112,128},... | collective-permute-start | bytes 6152 | tf_op jit(solution)/shard_map/ppermute | solution.py:19
  96.7 3.7 %collective-permute-start.18 = (f32[2,1,8,32]{3,2,1,0:T(8,128)S(1)}, f32[2,1,8,32]{3,2,1,0:T(8,128)S(1)}, u32[]{:S(2)}, u32[]{:S(2)}) collective-permute-start(f32[2,1,8,32]{3,2,1,0:T(8,128)S(1)} %slice.511), channel_id=1, source_target_pairs={{0,240},{16,0},{32,16},{48,32},{64,48},{80,64},{96,80},{112,96},{1... | collective-permute-start | bytes 6152 | tf_op jit(solution)/shard_map/ppermute | solution.py:19
  100.5 7.3 %collective-permute-start.19 = (f32[2,1,8,32]{3,2,1,0:T(8,128)S(1)}, f32[2,1,8,32]{3,2,1,0:T(8,128)S(1)}, u32[]{:S(2)}, u32[]{:S(2)}) collective-permute-start(f32[2,1,8,32]{3,2,1,0:T(8,128)S(1)} %slice.512), channel_id=1, source_target_pairs={{0,16},{16,32},{32,48},{48,64},{64,80},{80,96},{96,112},{112,128},... | collective-permute-start | bytes 6152 | tf_op jit(solution)/shard_map/ppermute | solution.py:19
  108.0 1.4 %collective-permute-start.20 = (f32[2,8,1,32]{3,2,1,0:T(1,128)S(1)}, f32[2,8,1,32]{3,2,1,0:T(1,128)S(1)}, u32[]{:S(2)}, u32[]{:S(2)}) collective-permute-start(f32[2,8,1,32]{3,2,1,0:T(1,128)S(1)} %slice.517), channel_id=1, source_target_pairs={{0,15},{1,0},{2,1},{3,2},{4,3},{5,4},{6,5},{7,6},{8,7},{9,8},{10,9... | collective-permute-start | bytes 6152 | tf_op jit(solution)/shard_map/ppermute | solution.py:19
  109.4 4.3 %collective-permute-start.21 = (f32[2,8,1,32]{3,2,1,0:T(1,128)S(1)}, f32[2,8,1,32]{3,2,1,0:T(1,128)S(1)}, u32[]{:S(2)}, u32[]{:S(2)}) collective-permute-start(f32[2,8,1,32]{3,2,1,0:T(1,128)S(1)} %slice.518), channel_id=1, source_target_pairs={{0,1},{1,2},{2,3},{3,4},{4,5},{5,6},{6,7},{7,8},{8,9},{9,10},{10,1... | collective-permute-start | bytes 6152 | tf_op jit(solution)/shard_map/ppermute | solution.py:19
  113.7 1.4 %collective-permute-start.22 = (f32[2,8,1,32]{3,2,1,0:T(1,128)S(1)}, f32[2,8,1,32]{3,2,1,0:T(1,128)S(1)}, u32[]{:S(2)}, u32[]{:S(2)}) collective-permute-start(f32[2,8,1,32]{3,2,1,0:T(1,128)S(1)} %slice.521), channel_id=1, source_target_pairs={{0,15},{1,0},{2,1},{3,2},{4,3},{5,4},{6,5},{7,6},{8,7},{9,8},{10,9... | collective-permute-start | bytes 6152 | tf_op jit(solution)/shard_map/ppermute | solution.py:19
  115.2 4.3 %collective-permute-start.23 = (f32[2,8,1,32]{3,2,1,0:T(1,128)S(1)}, f32[2,8,1,32]{3,2,1,0:T(1,128)S(1)}, u32[]{:S(2)}, u32[]{:S(2)}) collective-permute-start(f32[2,8,1,32]{3,2,1,0:T(1,128)S(1)} %slice.522), channel_id=1, source_target_pairs={{0,1},{1,2},{2,3},{3,4},{4,5},{5,6},{6,7},{7,8},{8,9},{9,10},{10,1... | collective-permute-start | bytes 6152 | tf_op jit(solution)/shard_map/ppermute | solution.py:19
where the time goes:
time: 126 us
  waiting for transfers between devices  85.9 us (68%)
  starting transfers between devices  17.2 us (14%)
  local copies, waits for them, and re-layouts  9.23 us (7%)
  other arithmetic  7.7 us (6%)
  matrix products  3.9 us (3%)
  between operations  1.67 us (1%)
    ppermute x24, waiting for transfers between devices, passed_along(): return lax.ppermute(value, axis, pairs)  85.9 us
    ppermute x24, starting transfers between devices, passed_along(): return lax.ppermute(value, axis, pairs)  17.2 us
    dot_general x6, matrix products, apply_last(): jnp.dot(flat, matrix, precision=lax.Precision.HIGHEST, preferred_element_...  3.9 us
  transfers between devices with their start and end apart: 24, of which 24 were waited for; matrix products, arithmetic and copies ran while one was open for 2% of the time, Pallas kernels for 0%

commit v1 on v0

v1 whole, which is shorter than its diff:
```python
import jax
import jax.numpy as jnp
import numpy as np
from jax import lax
from jax.experimental import pallas as pl
from jax.experimental.pallas import tpu as pltpu
from jax.sharding import PartitionSpec as P

LEVELS = 3
LIFT_ALPHA = -1.586134342
LIFT_BETA = -0.05298011854
LIFT_GAMMA = 0.8829110762
LIFT_DELTA = 0.4435068522
LIFT_KAPPA = 1.149604398
MESH = pl.DeviceIdType.MESH
N = 32
NZ = 128
EDGE_ROWS = 208
CORNER_ROWS = 48


def lift_matrix(count, periodic):
    eye = np.eye(count)
    even, odd = eye[0::2], eye[1::2]
    if periodic:
        following = lambda t: np.roll(t, -1, 0)
        before = lambda t: np.roll(t, 1, 0)
    else:
        following = lambda t: np.concatenate([t[1:], t[-1:]])
        before = lambda t: np.concatenate([t[:1], t[:-1]])
    odd = odd + LIFT_ALPHA * (even + following(even))
    even = even + LIFT_BETA * (before(odd) + odd)
    odd = odd + LIFT_GAMMA * (even + following(even))
    even = even + LIFT_DELTA * (before(odd) + odd)
    out = np.zeros((count, count))
    out[0::2], out[1::2] = even / LIFT_KAPPA, odd * LIFT_KAPPA
    return out


def factor(matrix, rank):
    u, s, vt = np.linalg.svd(matrix)
    assert s[rank:].max() < 1e-12
    return u[:, :rank] * s[:rank], vt[:rank]


def axis_operators():
    found, current = [], np.eye(5 * N)
    for level, (up, down) in enumerate(((2, 2), (3, 3), (4, 3))):
        full = lift_matrix(current.shape[0], True) @ current
        size = N >> level
        rows = full[2 * size : 3 * size]
        gain_left, send_up = factor(rows[:, N : 2 * N], up)
        gain_right, send_down = factor(rows[:, 3 * N : 4 * N], down)
        found.append((rows[:, 2 * N : 3 * N], send_up, send_down, gain_left, gain_right))
        current = full[0::2]
    return found


def depth_operators():
    one = lift_matrix(NZ, False)
    two = lift_matrix(NZ // 2, False) @ one[0::2]
    three = lift_matrix(NZ // 4, False) @ two[0::2]
    return one, two, three


OPS = axis_operators()


def padded(matrix, rows):
    return np.concatenate([matrix, np.zeros((rows - matrix.shape[0],) + matrix.shape[1:])])


def blocks(matrix, count):
    return np.kron(np.eye(count), matrix)


def batched(matrix):
    rows, cols = matrix.shape
    out = np.zeros((rows, 8, 8, cols))
    for i in range(8):
        out[:, i, i, :] = matrix
    return out.reshape(rows * 8, 8 * cols)


def corner_matrix(up, down, count, rows):
    out = np.zeros((4, rows, 2 * count, N))
    for corner in range(4):
        for jy in range(count):
            for jx, line in enumerate((up, down)[corner // 2]):
                out[corner, count * jy + jx, count * (corner % 2) + jy] = line
    return out.reshape(4 * rows, 2 * count * N)


def gain_matrix(level, states):
    _, _, _, left, right = OPS[level]
    size = N >> level
    left4 = np.zeros((size, 4))
    right4 = np.zeros((size, 4))
    left4[:, : left.shape[1]] = left
    right4[:, : right.shape[1]] = right
    eye = np.eye(size)
    parts = []
    for gain in (left4, right4):
        parts.append(np.einsum("xj,yv->xyjv", gain[:, :states], eye).reshape(size * size, -1))
    for gain in (left4, right4):
        parts.append(np.einsum("yj,xv->xyjv", gain[:, :states], eye).reshape(size * size, -1))
    for corner in range(4):
        gx = (left4, right4)[corner // 2]
        gy = (left4, right4)[corner % 2]
        parts.append(np.einsum("xi,yj->xyji", gx, gy).reshape(size * size, 16))
    out = np.concatenate(parts, 1)
    return np.pad(out, ((0, 0), (0, 256 - out.shape[1])))


def halves(matrix):
    high = np.asarray(matrix, jnp.bfloat16)
    low = np.asarray(matrix - high.astype(np.float64), jnp.bfloat16)
    return high, low


def wide(matrix):
    return np.pad(matrix, ((0, 0), (0, 256 - matrix.shape[1])))


def tables():
    one, two, three = depth_operators()
    depth = np.zeros((2, NZ, 256))
    for f in range(2):
        depth[f, :, 64 * f : 64 * f + 64] = two.T
        depth[f, :, 128 + 32 * f : 160 + 32 * f] = three.T
    own1, up1, down1, _, _ = OPS[0]
    own2, up2, down2, _, _ = OPS[1]
    own3, up3, down3, _, _ = OPS[2]
    ext2 = np.concatenate([own2, padded(up2, 4), padded(down2, 4)])
    ext3 = np.concatenate([own3, up3, padded(down3, 4)])
    spread2 = np.zeros((2, 64, 2, NZ))
    spread3 = np.zeros((4, 32, 2, NZ))
    for f in range(2):
        for i in range(64):
            spread2[f, i, f, 2 * i] = 1
        for i in range(32):
            spread3[f, i, f, 4 * i] = 1
    pairs = {}
    pairs["z1"] = one.T
    pairs["x1"] = blocks(own1, 4)
    pairs["c1"] = corner_matrix(up1, down1, 2, 8)
    pairs["z23"] = depth.reshape(256, 256)
    pairs["s1"] = batched(np.concatenate([up1, down1]))
    pairs["b2"] = batched(ext2)
    pairs["n2"] = blocks(own2, 8)
    pairs["c2"] = corner_matrix(up2, down2, 4, 16)
    pairs["b3"] = batched(ext3)
    pairs["n3"] = blocks(own3, 8)
    pairs["c3"] = corner_matrix(up3, down3, 4, 16)
    pairs["m2"] = gain_matrix(1, 3)
    pairs["m3"] = gain_matrix(2, 4)
    packed, where, at = [], {}, 0

    def put(name, array):
        nonlocal at
        where[name] = (at, array.shape[0])
        packed.append(array)
        at += array.shape[0]

    for name, matrix in pairs.items():
        high, low = halves(matrix)
        if matrix.shape[1] == 128:
            put(name, np.concatenate([high, low], 1))
        else:
            put(name + "h", high)
            put(name + "l", low)
    high, low = halves(blocks(own1, 2))
    put("u1", wide(np.concatenate([high, high, low], 1)))
    put("p2", np.asarray(spread2.reshape(128, 256), jnp.bfloat16))
    put("p3", np.asarray(spread3.reshape(128, 256), jnp.bfloat16))
    return np.concatenate(packed), where


TABLE, WHERE = tables()


def split(value):
    high = value.astype(jnp.bfloat16)
    return high, (value - high.astype(jnp.float32)).astype(jnp.bfloat16)


def dot(a, b):
    return jnp.dot(a, b, preferred_element_type=jnp.float32)


def column(gain, first):
    row = lax.broadcasted_iota(jnp.int32, (8, NZ), 0)
    out = jnp.zeros((8, NZ), jnp.float32)
    for i in range(8):
        if abs(gain[first + i]) > 1e-13:
            out = jnp.where(row == i, jnp.float32(gain[first + i]), out)
    return out


def lift_own(lines):
    pairs = N // 2
    even = lines[0::2]
    odd = lines[1::2]
    zero = jnp.zeros_like(even[0])
    odd = [LIFT_ALPHA * even[0]] + [odd[i] + LIFT_ALPHA * (even[i] + (even[i + 1] if i + 1 < pairs else zero)) for i in range(pairs)]
    even = [LIFT_BETA * odd[0]] + [even[i] + LIFT_BETA * (odd[i] + odd[i + 1]) for i in range(pairs)] + [LIFT_BETA * odd[pairs]]
    odd = [odd[i] + LIFT_GAMMA * (even[i] + even[i + 1]) for i in range(pairs + 1)]
    out = []
    for i in range(pairs):
        out.append((even[i + 1] + LIFT_DELTA * (odd[i] + odd[i + 1])) * (1.0 / LIFT_KAPPA))
        out.append(odd[i + 1] * LIFT_KAPPA)
    return out


def kernel(nx, ny, v0_ref, v1_ref, table_ref, out0_ref, out1_ref, fields, table, w1h, w1l, w2h, w2l, w3h, w3l, sides, states1, lines, states2, states3, level2, level3, send_edge, send_corner, got_edge, got_corner, in_sem, send_sem, recv_sem):
    ix, iy = lax.axis_index("dx"), lax.axis_index("dy")
    right, left = lax.rem(ix + 1, nx), lax.rem(ix + nx - 1, nx)
    above, below = lax.rem(iy + 1, ny), lax.rem(iy + ny - 1, ny)
    edge_to = [(right, iy), (left, iy), (ix, above), (ix, below)]
    corner_to = [(right, above), (right, below), (left, above), (left, below)]

    loads = [
        pltpu.make_async_copy(v0_ref, fields.at[0], in_sem.at[0]),
        pltpu.make_async_copy(v1_ref, fields.at[1], in_sem.at[1]),
        pltpu.make_async_copy(table_ref, table, in_sem.at[2]),
    ]
    for load in loads:
        load.start()
    barrier = pltpu.get_barrier_semaphore()
    for there in corner_to + edge_to:
        pl.semaphore_signal(barrier, inc=1, device_id=there, device_id_type=MESH)
    for load in loads:
        load.wait()

    def part(name):
        at, rows = WHERE[name]
        return table[at : at + rows, :]

    def both(name):
        if name in WHERE:
            return part(name)[:, :128], part(name)[:, 128:]
        return part(name + "h"), part(name + "l")

    def times(name, pair):
        (ah, al), (bh, bl) = both(name), pair
        return dot(ah, bh) + dot(ah, bl) + dot(al, bh)

    def timed(pair, name):
        (ah, al), (bh, bl) = pair, both(name)
        return dot(ah, bh) + dot(al, bh) + dot(ah, bl)

    for b in range(4):
        v0 = split(fields[0, 8 * b : 8 * b + 8].reshape(256, NZ))
        v1 = split(fields[1, 8 * b : 8 * b + 8].reshape(256, NZ))
        w1 = jnp.concatenate([timed(v0, "z1"), timed(v1, "z1")], 1)
        v01 = [jnp.concatenate([p, q], 1) for p, q in zip(v0, v1)]
        w23 = timed(v01, "z23")
        rows = slice(256 * b, 256 * b + 256)
        w1h[rows, :], w1l[rows, :] = split(w1)
        high, low = split(w23)
        w2h[rows, :], w3h[rows, :] = high[:, :128], high[:, 128:]
        w2l[rows, :], w3l[rows, :] = low[:, :128], low[:, 128:]
        if b == 0:
            for j in range(2):
                sides[2 + j] = sum(float(OPS[0][2][j, i]) * w1[32 * i : 32 * i + 32] for i in range(3))
        if b == 3:
            for j in range(2):
                sides[j] = sum(float(OPS[0][1][j, 28 + i]) * w1[128 + 32 * i : 160 + 32 * i] for i in range(4))

    for b in range(4):
        rows = slice(256 * b, 256 * b + 256)
        here = slice(8 * b, 8 * b + 8)
        states1[:, here, :] = times("s1", (w1h[rows, :], w1l[rows, :])).reshape(4, 8, 256)
        states2[:, here, :] = times("b2", (w2h[rows, :], w2l[rows, :])).reshape(24, 8, NZ)
        states3[:, here, :] = times("b3", (w3h[rows, :], w3l[rows, :])).reshape(16, 8, NZ)

    def put_edges1(first, value):
        for k in range(2):
            for f in range(2):
                send_edge[first + k, 64 * f : 64 * f + 64, :] = value[64 * k : 64 * k + 64, 128 * f : 128 * f + 128]

    lines1 = split(states1[...].reshape(128, 256))
    put_edges1(0, times("x1", split(sides[...].reshape(128, 256))))
    put_edges1(2, times("x1", lines1))
    corners1 = times("c1", lines1)
    for c in range(4):
        for f in range(2):
            send_corner[c, 8 * f : 8 * f + 8, :] = corners1[8 * c : 8 * c + 8, 128 * f : 128 * f + 128]

    for c in range(2):
        value = times("b2", split(states2[8 * c : 8 * c + 8].reshape(256, NZ))).reshape(24, 8, NZ)
        level2[:, 8 * c : 8 * c + 8, :] = value[:16]
        for k in range(2):
            for j in range(3):
                send_edge[k, 128 + 16 * j + 8 * c : 136 + 16 * j + 8 * c, :] = value[16 + 4 * k + j]
    lines2 = split(states2[16:24].reshape(256, NZ))
    value = times("n2", lines2)
    for k in range(2):
        send_edge[2 + k, 128:176, :] = value[64 * k : 64 * k + 48]
    value = times("c2", lines2)
    for c in range(4):
        send_corner[c, 16:32, :] = value[16 * c : 16 * c + 16]
    value = times("b3", split(states3[0:8].reshape(256, NZ))).reshape(16, 8, NZ)
    level3[...] = value[:8]
    for k in range(2):
        send_edge[k, 176:208, :] = value[8 + 4 * k : 12 + 4 * k].reshape(32, NZ)
    lines3 = split(states3[8:16].reshape(256, NZ))
    value = times("n3", lines3)
    for k in range(2):
        send_edge[2 + k, 176:208, :] = value[32 * k : 32 * k + 32]
    value = times("c3", lines3)
    for c in range(4):
        send_corner[c, 32:48, :] = value[16 * c : 16 * c + 16]

    pl.semaphore_wait(barrier, 8)
    copies = []
    for c in range(4):
        copies.append(pltpu.make_async_remote_copy(src_ref=send_corner.at[c], dst_ref=got_corner.at[c], send_sem=send_sem.at[c], recv_sem=recv_sem.at[c], device_id=corner_to[c], device_id_type=MESH))
    for k in range(4):
        copies.append(pltpu.make_async_remote_copy(src_ref=send_edge.at[k], dst_ref=got_edge.at[k], send_sem=send_sem.at[4 + k], recv_sem=recv_sem.at[4 + k], device_id=edge_to[k], device_id_type=MESH))
    for copy in copies:
        copy.start()

    outs = (out0_ref, out1_ref)
    own = part("u1")[:, :192]
    for p in range(16):
        rows = slice(64 * p, 64 * p + 64)
        high = w1h[rows, :]
        value = dot(own, jnp.concatenate([high, w1l[rows, :], high], 0))
        lines[2 * p] = value[:32]
        lines[2 * p + 1] = value[32:]
    for f in range(2):
        for t in range(4):
            value = lift_own([lines[i, 8 * t : 8 * t + 8, 128 * f : 128 * f + 128] for i in range(N)])
            for i in range(N):
                outs[f][i, 8 * t : 8 * t + 8, :] = value[i]

    for copy in copies:
        copy.wait()

    parts2 = [got_edge[k, 128:176, :] for k in range(4)] + [got_corner[c, 16:32, :] for c in range(4)]
    value2 = times("m2", split(jnp.concatenate(parts2, 0))) + level2[...].reshape(256, NZ)
    parts3 = [got_edge[k, 176:208, :] for k in range(4)] + [got_corner[c, 32:48, :] for c in range(4)]
    parts3.append(jnp.zeros((64, NZ), jnp.float32))
    value3 = times("m3", split(jnp.concatenate(parts3, 0))) + level3[...].reshape(64, NZ)
    high, low = split(value2)
    value2 = dot(high, part("p2")) + dot(low, part("p2"))
    high, low = split(value3)
    value3 = dot(high, part("p3")) + dot(low, part("p3"))

    gains = (OPS[0][3], OPS[0][4])
    for f in range(2):
        for k, xs in enumerate(((0, 1, 2), (28, 29, 30, 31))):
            for x in xs:
                outs[f][x] += sum(float(gains[k][x, j]) * got_edge[k, 64 * f + 32 * j : 64 * f + 32 * j + 32, :] for j in range(2))
        for k in range(2):
            for j in range(2):
                for side, first in enumerate((0, 24)):
                    at = 64 * f + 32 * j + first
                    corner = 2 * side + k
                    more = [column(gains[side][:, i], first) * got_corner[corner, 8 * f + 2 * j + i : 8 * f + 2 * j + i + 1, :] for i in range(2)]
                    got_edge[2 + k, at : at + 8, :] += more[0] + more[1]
        for k, first in enumerate((0, 24)):
            cols = [column(gains[k][:, j], first) for j in range(2)]
            for x in range(N):
                outs[f][x, first : first + 8, :] += sum(cols[j] * got_edge[2 + k, 64 * f + 32 * j + x : 64 * f + 32 * j + x + 1, :] for j in range(2))

    lane = lax.broadcasted_iota(jnp.int32, (16, NZ), 1)
    for f in range(2):
        for x in range(16):
            old = outs[f][2 * x, pl.ds(0, 16, stride=2), :]
            outs[f][2 * x, pl.ds(0, 16, stride=2), :] = jnp.where(lane % 2 == 0, value2[16 * x : 16 * x + 16, 128 * f : 128 * f + 128], old)
        for x in range(8):
            old = outs[f][4 * x, pl.ds(0, 8, stride=4), :]
            outs[f][4 * x, pl.ds(0, 8, stride=4), :] = jnp.where(lane[:8] % 4 == 0, value3[8 * x : 8 * x + 8, 128 * f : 128 * f + 128], old)


def solution(mesh):
    nx, ny = mesh.shape["dx"], mesh.shape["dy"]

    def body(volume_fraction, vorticity):
        block = jax.ShapeDtypeStruct((N, N, NZ), jnp.float32)
        f32, bf16 = jnp.float32, jnp.bfloat16
        return pl.pallas_call(
            lambda *refs: kernel(nx, ny, *refs),
            out_shape=(block, block),
            in_specs=[pl.BlockSpec(memory_space=pl.ANY)] * 3,
            out_specs=(pl.BlockSpec(memory_space=pltpu.VMEM),) * 2,
            scratch_shapes=[
                pltpu.VMEM((2, N, N, NZ), f32),
                pltpu.VMEM(TABLE.shape, bf16),
                pltpu.VMEM((1024, 256), bf16),
                pltpu.VMEM((1024, 256), bf16),
                pltpu.VMEM((1024, NZ), bf16),
                pltpu.VMEM((1024, NZ), bf16),
                pltpu.VMEM((1024, NZ), bf16),
                pltpu.VMEM((1024, NZ), bf16),
                pltpu.VMEM((4, N, 256), f32),
                pltpu.VMEM((4, N, 256), f32),
                pltpu.VMEM((N, N, 256), f32),
                pltpu.VMEM((24, N, NZ), f32),
                pltpu.VMEM((16, N, NZ), f32),
                pltpu.VMEM((16, 16, NZ), f32),
                pltpu.VMEM((8, 8, NZ), f32),
                pltpu.VMEM((4, EDGE_ROWS, NZ), f32),
                pltpu.VMEM((4, CORNER_ROWS, NZ), f32),
                pltpu.VMEM((4, EDGE_ROWS, NZ), f32),
                pltpu.VMEM((4, CORNER_ROWS, NZ), f32),
                pltpu.SemaphoreType.DMA((3,)),
                pltpu.SemaphoreType.DMA((8,)),
                pltpu.SemaphoreType.DMA((8,)),
            ],
            compiler_params=pltpu.CompilerParams(
                collective_id=0, has_side_effects=True, vmem_limit_bytes=32 * 1024 * 1024
            ),
        )(volume_fraction, vorticity, jnp.asarray(TABLE))

    placed = P("dx", "dy", None)
    return jax.shard_map(
        body, mesh=mesh, in_specs=(placed, placed), out_specs=(placed, placed), check_vma=False
    )
```

time: 126 us -> 20.5 us (0.16)
  the two profiles are of different devices: /device:TPU:0 before, /device:TPU:2 now
where the time goes in v1:
time: 20.5 us; the launch traced here: 20.3 us
  Pallas kernels  14.6 us (71%)
  local copies, waits for them, and re-layouts  5.08 us (25%)
  between operations  0.65 us (3%)
    pallas_call x1, Pallas kernels, body(): pl.pallas_call(lambda *refs: kernel(nx, ny, *refs), out_shape=(block, blo...  14.6 us
    unnamed x8, local copies, waits for them, and re-layouts  5.08 us

profile of v1, /device:TPU:2, one launch (start us, length us, event | category | flops | bytes accessed | tf_op | source)
XLA Modules:
  0.0 20.3 jit_solution(16152428003296621921)
XLA Ops:
  0.6 0.0 copy-start
  0.6 1.4 %copy-done = bf16[3104,256]{1,0:T(8,128)(2,1)S(1)} copy-done((bf16[3104,256]{1,0:T(8,128)(2,1)S(1)}, bf16[3104,256]{1,0:T(8,128)(2,1)}, u32[]{:S(2)}) %copy-start) | copy-done | bytes 1589272
  2.0 0.0 copy-start.1
  2.0 1.0 %copy-done.1 = f32[32,32,128]{2,1,0:T(8,128)S(1)} copy-done((f32[32,32,128]{2,1,0:T(8,128)S(1)}, f32[32,32,128]{2,1,0:T(8,128)}, u32[]{:S(2)}) %copy-start.1) | copy-done | bytes 524312
  3.1 0.0 copy-start.2
  3.1 1.0 %copy-done.2 = f32[32,32,128]{2,1,0:T(8,128)S(1)} copy-done((f32[32,32,128]{2,1,0:T(8,128)S(1)}, f32[32,32,128]{2,1,0:T(8,128)}, u32[]{:S(2)}) %copy-start.2) | copy-done | bytes 524312
  4.1 14.6 %shard_map.50 = (f32[32,32,128]{2,1,0:T(8,128)S(1)}, f32[32,32,128]{2,1,0:T(8,128)S(1)}) custom-call(f32[32,32,128]{2,1,0:T(8,128)S(1)} %copy-done.1, f32[32,32,128]{2,1,0:T(8,128)S(1)} %copy-done.2, bf16[3104,256]{1,0:T(8,128)(2,1)S(1)} %copy-done), custom_call_target="tpu_custom_call" | custom-call | tf_op jit(solution)/shard_map/pallas_call | solution.py:384
  18.7 0.8 %copy.7 = f32[32,32,128]{2,1,0:T(8,128)} copy(f32[32,32,128]{2,1,0:T(8,128)S(1)} %get-tuple-element.4) | data formatting | bytes 1048576
  19.5 0.8 %copy.8 = f32[32,32,128]{2,1,0:T(8,128)} copy(f32[32,32,128]{2,1,0:T(8,128)S(1)} %get-tuple-element.5) | data formatting | bytes 1048576
Async XLA Ops:
  0.6 1.4 %copy-start = (bf16[3104,256]{1,0:T(8,128)(2,1)S(1)}, bf16[3104,256]{1,0:T(8,128)(2,1)}, u32[]{:S(2)}) copy-start(bf16[3104,256]{1,0:T(8,128)(2,1)} %constant.2.clone.refs_2_) | copy-start | bytes 4767748
  2.0 1.0 %copy-start.1 = (f32[32,32,128]{2,1,0:T(8,128)S(1)}, f32[32,32,128]{2,1,0:T(8,128)}, u32[]{:S(2)}) copy-start(f32[32,32,128]{2,1,0:T(8,128)} %refs_0_.1) | copy-start | bytes 1572868
  3.1 1.0 %copy-start.2 = (f32[32,32,128]{2,1,0:T(8,128)S(1)}, f32[32,32,128]{2,1,0:T(8,128)}, u32[]{:S(2)}) copy-start(f32[32,32,128]{2,1,0:T(8,128)} %refs_1_.1) | copy-start | bytes 1572868

commit v2 on v1

--- a/solution.py
+++ b/solution.py
@@ -154,13 +154,14 @@
     pairs["c3"] = corner_matrix(up3, down3, 4, 16)
     pairs["m2"] = gain_matrix(1, 3)
     pairs["m3"] = gain_matrix(2, 4)
-    packed, where, at = [], {}, 0
+    groups = (("z1", "z23"), ("x1", "c1", "s1", "b2", "n2", "c2", "b3", "n3", "c3", "u1"), ("m2", "m3", "p2", "p3"))
+    packed, where, at = [[], [], []], {}, [0, 0, 0]
 
     def put(name, array):
-        nonlocal at
-        where[name] = (at, array.shape[0])
-        packed.append(array)
-        at += array.shape[0]
+        group = next(i for i, names in enumerate(groups) if name in names or name[:-1] in names)
+        where[name] = (group, at[group], array.shape[0])
+        packed[group].append(array)
+        at[group] += array.shape[0]
 
     for name, matrix in pairs.items():
         high, low = halves(matrix)
@@ -173,10 +174,10 @@
     put("u1", wide(np.concatenate([high, high, low], 1)))
     put("p2", np.asarray(spread2.reshape(128, 256), jnp.bfloat16))
     put("p3", np.asarray(spread3.reshape(128, 256), jnp.bfloat16))
-    return np.concatenate(packed), where
-
-
-TABLE, WHERE = tables()
+    return [np.concatenate(group) for group in packed], where
+
+
+TABLES, WHERE = tables()
 
 
 def split(value):
@@ -212,7 +213,28 @@
     return out
 
 
-def kernel(nx, ny, v0_ref, v1_ref, table_ref, out0_ref, out1_ref, fields, table, w1h, w1l, w2h, w2l, w3h, w3l, sides, states1, lines, states2, states3, level2, level3, send_edge, send_corner, got_edge, got_corner, in_sem, send_sem, recv_sem):
+def reader(*refs):
+    def part(name):
+        group, at, rows = WHERE[name]
+        return refs[group][at : at + rows, :]
+
+    def both(name):
+        if name in WHERE:
+            return part(name)[:, :128], part(name)[:, 128:]
+        return part(name + "h"), part(name + "l")
+
+    def times(name, pair):
+        (ah, al), (bh, bl) = both(name), pair
+        return dot(ah, bh) + dot(ah, bl) + dot(al, bh)
+
+    def timed(pair, name):
+        (ah, al), (bh, bl) = pair, both(name)
+        return dot(ah, bh) + dot(al, bh) + dot(ah, bl)
+
+    return part, times, timed
+
+
+def exchange(nx, ny, v0_ref, v1_ref, table0_ref, table1_ref, table2_ref, got_edge, got_corner, own1, level2, level3, table2, fields, table0, table1, w1h, w1l, w2h, w2l, w3h, w3l, sides, states1, lines, states2, states3, send_edge, send_corner, in_sem, send_sem, recv_sem):
     ix, iy = lax.axis_index("dx"), lax.axis_index("dy")
     right, left = lax.rem(ix + 1, nx), lax.rem(ix + nx - 1, nx)
     above, below = lax.rem(iy + 1, ny), lax.rem(iy + ny - 1, ny)
@@ -222,32 +244,18 @@
     loads = [
         pltpu.make_async_copy(v0_ref, fields.at[0], in_sem.at[0]),
         pltpu.make_async_copy(v1_ref, fields.at[1], in_sem.at[1]),
-        pltpu.make_async_copy(table_ref, table, in_sem.at[2]),
+        pltpu.make_async_copy(table0_ref, table0, in_sem.at[2]),
+        pltpu.make_async_copy(table1_ref, table1, in_sem.at[3]),
+        pltpu.make_async_copy(table2_ref, table2, in_sem.at[4]),
     ]
     for load in loads:
         load.start()
     barrier = pltpu.get_barrier_semaphore()
     for there in corner_to + edge_to:
         pl.semaphore_signal(barrier, inc=1, device_id=there, device_id_type=MESH)
-    for load in loads:
+    part, times, timed = reader(table0, table1)
+    for load in loads[:3]:
         load.wait()
-
-    def part(name):
-        at, rows = WHERE[name]
-        return table[at : at + rows, :]
-
-    def both(name):
-        if name in WHERE:
-            return part(name)[:, :128], part(name)[:, 128:]
-        return part(name + "h"), part(name + "l")
-
-    def times(name, pair):
-        (ah, al), (bh, bl) = both(name), pair
-        return dot(ah, bh) + dot(ah, bl) + dot(al, bh)
-
-    def timed(pair, name):
-        (ah, al), (bh, bl) = pair, both(name)
-        return dot(ah, bh) + dot(al, bh) + dot(ah, bl)
 
     for b in range(4):
         v0 = split(fields[0, 8 * b : 8 * b + 8].reshape(256, NZ))
@@ -267,6 +275,7 @@
             for j in range(2):
                 sides[j] = sum(float(OPS[0][1][j, 28 + i]) * w1[128 + 32 * i : 160 + 32 * i] for i in range(4))
 
+    loads[3].wait()
     for b in range(4):
         rows = slice(256 * b, 256 * b + 256)
         here = slice(8 * b, 8 * b + 8)
@@ -321,7 +330,6 @@
     for copy in copies:
         copy.start()
 
-    outs = (out0_ref, out1_ref)
     own = part("u1")[:, :192]
     for p in range(16):
         rows = slice(64 * p, 64 * p + 64)
@@ -333,10 +341,15 @@
         for t in range(4):
             value = lift_own([lines[i, 8 * t : 8 * t + 8, 128 * f : 128 * f + 128] for i in range(N)])
             for i in range(N):
-                outs[f][i, 8 * t : 8 * t + 8, :] = value[i]
-
+                own1[f, i, 8 * t : 8 * t + 8, :] = value[i]
+
+    loads[4].wait()
     for copy in copies:
         copy.wait()
+
+
+def finish(got_edge, got_corner, own1, level2, level3, table2, out0_ref, out1_ref, out, lines, out_sem):
+    part, times, _ = reader(None, None, table2)
 
     parts2 = [got_edge[k, 128:176, :] for k in range(4)] + [got_corner[c, 16:32, :] for c in range(4)]
     value2 = times("m2", split(jnp.concatenate(parts2, 0))) + level2[...].reshape(256, NZ)
@@ -349,46 +362,76 @@
     value3 = dot(high, part("p3")) + dot(low, part("p3"))
 
     gains = (OPS[0][3], OPS[0][4])
+    lane = lax.broadcasted_iota(jnp.int32, (16, NZ), 1)
+    stores = []
     for f in range(2):
-        for k, xs in enumerate(((0, 1, 2), (28, 29, 30, 31))):
-            for x in xs:
-                outs[f][x] += sum(float(gains[k][x, j]) * got_edge[k, 64 * f + 32 * j : 64 * f + 32 * j + 32, :] for j in range(2))
+        ends = []
         for k in range(2):
+            ends.append([])
             for j in range(2):
-                for side, first in enumerate((0, 24)):
-                    at = 64 * f + 32 * j + first
+                at = 64 * f + 32 * j
+                rows = [got_edge[2 + k, at + 8 * t : at + 8 * t + 8, :] for t in range(4)]
+                for side, t in enumerate((0, 3)):
                     corner = 2 * side + k
-                    more = [column(gains[side][:, i], first) * got_corner[corner, 8 * f + 2 * j + i : 8 * f + 2 * j + i + 1, :] for i in range(2)]
-                    got_edge[2 + k, at : at + 8, :] += more[0] + more[1]
-        for k, first in enumerate((0, 24)):
-            cols = [column(gains[k][:, j], first) for j in range(2)]
-            for x in range(N):
-                outs[f][x, first : first + 8, :] += sum(cols[j] * got_edge[2 + k, 64 * f + 32 * j + x : 64 * f + 32 * j + x + 1, :] for j in range(2))
-
-    lane = lax.broadcasted_iota(jnp.int32, (16, NZ), 1)
-    for f in range(2):
-        for x in range(16):
-            old = outs[f][2 * x, pl.ds(0, 16, stride=2), :]
-            outs[f][2 * x, pl.ds(0, 16, stride=2), :] = jnp.where(lane % 2 == 0, value2[16 * x : 16 * x + 16, 128 * f : 128 * f + 128], old)
-        for x in range(8):
-            old = outs[f][4 * x, pl.ds(0, 8, stride=4), :]
-            outs[f][4 * x, pl.ds(0, 8, stride=4), :] = jnp.where(lane[:8] % 4 == 0, value3[8 * x : 8 * x + 8, 128 * f : 128 * f + 128], old)
+                    for i in range(2):
+                        rows[t] += column(gains[side][:, i], 8 * t) * got_corner[corner, 8 * f + 2 * j + i : 8 * f + 2 * j + i + 1, :]
+                for t in range(4):
+                    lines[k, j, 8 * t : 8 * t + 8, :] = rows[t]
+        cols = [[column(gains[k][:, j], 24 * k) for j in range(2)] for k in range(2)]
+        for x in range(N):
+            value = [own1[f, x, 8 * t : 8 * t + 8, :] for t in range(4)]
+            for k, xs in enumerate(((0, 1, 2), (28, 29, 30, 31))):
+                if x in xs:
+                    for j in range(2):
+                        for t in range(4):
+                            at = 64 * f + 32 * j + 8 * t
+                            value[t] += float(gains[k][x, j]) * got_edge[k, at : at + 8, :]
+            for k in range(2):
+                for j in range(2):
+                    value[3 * k] += cols[k][j] * lines[k, j, x : x + 1, :]
+            for t in range(4):
+                out[f, x, 8 * t : 8 * t + 8, :] = value[t]
+            if x % 2 == 0:
+                at = 8 * x
+                cells = out[f, x, pl.ds(0, 16, stride=2), :]
+                out[f, x, pl.ds(0, 16, stride=2), :] = jnp.where(lane % 2 == 0, value2[at : at + 16, 128 * f : 128 * f + 128], cells)
+            if x % 4 == 0:
+                at = 2 * x
+                cells = out[f, x, pl.ds(0, 8, stride=4), :]
+                out[f, x, pl.ds(0, 8, stride=4), :] = jnp.where(lane[:8] % 4 == 0, value3[at : at + 8, 128 * f : 128 * f + 128], cells)
+            if x % 16 == 15:
+                here = pl.ds(x - 15, 16)
+                store = pltpu.make_async_copy(out.at[f, here], (out0_ref, out1_ref)[f].at[here], out_sem.at[2 * f + x // 16])
+                store.start()
+                stores.append(store)
+    for store in stores:
+        store.wait()
 
 
 def solution(mesh):
     nx, ny = mesh.shape["dx"], mesh.shape["dy"]
+    f32, bf16 = jnp.float32, jnp.bfloat16
 
     def body(volume_fraction, vorticity):
-        block = jax.ShapeDtypeStruct((N, N, NZ), jnp.float32)
-        f32, bf16 = jnp.float32, jnp.bfloat16
-        return pl.pallas_call(
-            lambda *refs: kernel(nx, ny, *refs),
-            out_shape=(block, block),
-            in_specs=[pl.BlockSpec(memory_space=pl.ANY)] * 3,
-            out_specs=(pl.BlockSpec(memory_space=pltpu.VMEM),) * 2,
+        inputs = [volume_fraction, vorticity] + [jnp.asarray(table) for table in TABLES]
+        inputs = [pltpu.with_memory_space_constraint(value, pltpu.HBM) for value in inputs]
+        passed = (
+            pltpu.VMEM((4, EDGE_ROWS, NZ), f32),
+            pltpu.VMEM((4, CORNER_ROWS, NZ), f32),
+            pltpu.VMEM((2, N, N, NZ), f32),
+            pltpu.VMEM((16, 16, NZ), f32),
+            pltpu.VMEM((8, 8, NZ), f32),
+            pltpu.VMEM(TABLES[2].shape, bf16),
+        )
+        middle = pl.pallas_call(
+            lambda *refs: exchange(nx, ny, *refs),
+            out_shape=passed,
+            in_specs=[pl.BlockSpec(memory_space=pltpu.HBM)] * 5,
+            out_specs=(pl.BlockSpec(memory_space=pltpu.VMEM),) * 6,
             scratch_shapes=[
                 pltpu.VMEM((2, N, N, NZ), f32),
-                pltpu.VMEM(TABLE.shape, bf16),
+                pltpu.VMEM(TABLES[0].shape, bf16),
+                pltpu.VMEM(TABLES[1].shape, bf16),
                 pltpu.VMEM((1024, 256), bf16),
                 pltpu.VMEM((1024, 256), bf16),
                 pltpu.VMEM((1024, NZ), bf16),
@@ -400,20 +443,30 @@
                 pltpu.VMEM((N, N, 256), f32),
                 pltpu.VMEM((24, N, NZ), f32),
                 pltpu.VMEM((16, N, NZ), f32),
-                pltpu.VMEM((16, 16, NZ), f32),
-                pltpu.VMEM((8, 8, NZ), f32),
                 pltpu.VMEM((4, EDGE_ROWS, NZ), f32),
                 pltpu.VMEM((4, CORNER_ROWS, NZ), f32),
-                pltpu.VMEM((4, EDGE_ROWS, NZ), f32),
-                pltpu.VMEM((4, CORNER_ROWS, NZ), f32),
-                pltpu.SemaphoreType.DMA((3,)),
+                pltpu.SemaphoreType.DMA((5,)),
                 pltpu.SemaphoreType.DMA((8,)),
                 pltpu.SemaphoreType.DMA((8,)),
             ],
             compiler_params=pltpu.CompilerParams(
                 collective_id=0, has_side_effects=True, vmem_limit_bytes=32 * 1024 * 1024
             ),
-        )(volume_fraction, vorticity, jnp.asarray(TABLE))
+        )(*inputs)
+        middle = [pltpu.with_memory_space_constraint(value, pltpu.VMEM) for value in middle]
+        block = pltpu.HBM((N, N, NZ), f32)
+        return pl.pallas_call(
+            finish,
+            out_shape=(block, block),
+            in_specs=[pl.BlockSpec(memory_space=pltpu.VMEM)] * 6,
+            out_specs=(pl.BlockSpec(memory_space=pltpu.HBM),) * 2,
+            scratch_shapes=[
+                pltpu.VMEM((2, N, N, NZ), f32),
+                pltpu.VMEM((2, 2, N, NZ), f32),
+                pltpu.SemaphoreType.DMA((4,)),
+            ],
+            compiler_params=pltpu.CompilerParams(vmem_limit_bytes=32 * 1024 * 1024),
+        )(*middle)
 
     placed = P("dx", "dy", None)
     return jax.shard_map(

time: 20.5 us -> 16.3 us (0.80)
  the two profiles are of different devices: /device:TPU:2 before, /device:TPU:0 now
where the time goes in v2:
time: 16.3 us; the launch traced here: 16 us
  Pallas kernels  15.3 us (94%)
  between operations  0.64 us (4%)
    pallas_call x1, Pallas kernels, body(): pl.pallas_call(lambda *refs: exchange(nx, ny, *refs), out_shape=passed, i...  13.8 us
    pallas_call x1, Pallas kernels, body(): pl.pallas_call(finish, out_shape=(block, block), in_specs=[pl.BlockSpec(m...  1.49 us

profile of v2, /device:TPU:0, one launch (start us, length us, event | category | flops | bytes accessed | tf_op | source)
XLA Modules:
  0.0 16.0 jit_solution(8482241508828289742)
XLA Ops:
  0.6 13.8 %shard_map.68 = (f32[4,208,128]{2,1,0:T(8,128)S(1)}, f32[4,48,128]{2,1,0:T(8,128)S(1)}, f32[2,32,32,128]{3,2,1,0:T(8,128)S(1)}, f32[16,16,128]{2,1,0:T(8,128)S(1...) custom-call(f32[32,32,128]{2,1,0:T(8,128)} %refs_0_.1, f32[32,32,128]{2,1,0:T(8,128)} %refs_1_.1, ...), custom_call_target="tpu_custom_call" | custom-call | tf_op jit(solution)/shard_map/pallas_call | solution.py:426
  14.5 1.5 %shard_map.69 = (f32[32,32,128]{2,1,0:T(8,128)}, f32[32,32,128]{2,1,0:T(8,128)}) custom-call(f32[4,208,128]{2,1,0:T(8,128)S(1)} %get-tuple-element.8.got_edge, f32[4,48,128]{2,1,0:T(8,128)S(1)} %get-tuple-element.9.got_corner, f32[2,32,32,128]{3,2,1,0:T(8,128)S(1)} %get-tuple-element.10.own1, f32[16,16,128]{2,1,0:T(8,128)S(1)} %get-tuple-element.11.level2, ...), custom_call_target="tpu_custom_call" | custom-call | tf_op jit(solution)/shard_map/pallas_call | solution.py:458

commit v3 on v2

v3 whole, which is shorter than its diff:
```python
import jax
import jax.numpy as jnp
import numpy as np
from jax import lax
from jax.experimental import pallas as pl
from jax.experimental.pallas import tpu as pltpu
from jax.sharding import PartitionSpec as P

LEVELS = 3
LIFT_ALPHA = -1.586134342
LIFT_BETA = -0.05298011854
LIFT_GAMMA = 0.8829110762
LIFT_DELTA = 0.4435068522
LIFT_KAPPA = 1.149604398
MESH = pl.DeviceIdType.MESH
N = 32
NZ = 128
EDGE_ROWS = 208
CORNER_ROWS = 48


def lift_matrix(count, periodic):
    eye = np.eye(count)
    even, odd = eye[0::2], eye[1::2]
    if periodic:
        following = lambda t: np.roll(t, -1, 0)
        before = lambda t: np.roll(t, 1, 0)
    else:
        following = lambda t: np.concatenate([t[1:], t[-1:]])
        before = lambda t: np.concatenate([t[:1], t[:-1]])
    odd = odd + LIFT_ALPHA * (even + following(even))
    even = even + LIFT_BETA * (before(odd) + odd)
    odd = odd + LIFT_GAMMA * (even + following(even))
    even = even + LIFT_DELTA * (before(odd) + odd)
    out = np.zeros((count, count))
    out[0::2], out[1::2] = even / LIFT_KAPPA, odd * LIFT_KAPPA
    return out


def factor(matrix, rank):
    u, s, vt = np.linalg.svd(matrix)
    assert s[rank:].max() < 1e-12
    return u[:, :rank] * s[:rank], vt[:rank]


def axis_operators():
    found, current = [], np.eye(5 * N)
    for level, (up, down) in enumerate(((2, 2), (3, 3), (4, 3))):
        full = lift_matrix(current.shape[0], True) @ current
        size = N >> level
        rows = full[2 * size : 3 * size]
        gain_left, send_up = factor(rows[:, N : 2 * N], up)
        gain_right, send_down = factor(rows[:, 3 * N : 4 * N], down)
        found.append((rows[:, 2 * N : 3 * N], send_up, send_down, gain_left, gain_right))
        current = full[0::2]
    return found


def depth_operators():
    one = lift_matrix(NZ, False)
    two = lift_matrix(NZ // 2, False) @ one[0::2]
    three = lift_matrix(NZ // 4, False) @ two[0::2]
    return one, two, three


OPS = axis_operators()


def padded(matrix, rows):
    return np.concatenate([matrix, np.zeros((rows - matrix.shape[0],) + matrix.shape[1:])])


def blocks(matrix, count):
    return np.kron(np.eye(count), matrix)


def batched(matrix):
    rows, cols = matrix.shape
    out = np.zeros((rows, 8, 8, cols))
    for i in range(8):
        out[:, i, i, :] = matrix
    return out.reshape(rows * 8, 8 * cols)


def corner_matrix(up, down, stride, rows):
    sent = (up, down)
    total = len(up) + len(down)
    out = np.zeros((4, rows, total, N))
    for corner in range(4):
        sx, sy = corner // 2, corner % 2
        for jy in range(len(sent[sy])):
            for jx, line in enumerate(sent[sx]):
                out[corner, stride * jy + jx, sy * len(up) + jy] = line
    return out.reshape(4 * rows, total * N)


def gain_matrix(level):
    gains = OPS[level][3:]
    size = N >> level
    eye = np.eye(size)
    parts = [np.einsum("xj,yv->xyjv", gain, eye).reshape(size * size, -1) for gain in gains]
    parts += [np.einsum("yj,xv->xyjv", gain, eye).reshape(size * size, -1) for gain in gains]
    four = [np.pad(gain, ((0, 0), (0, 4 - gain.shape[1]))) for gain in gains]
    for corner in range(4):
        parts.append(np.einsum("xi,yj->xyji", four[corner // 2], four[corner % 2]).reshape(size * size, 16))
    return wide(np.concatenate(parts, 1))


def halves(matrix):
    high = np.asarray(matrix, jnp.bfloat16)
    low = np.asarray(matrix - high.astype(np.float64), jnp.bfloat16)
    return high, low


def wide(matrix):
    return np.pad(matrix, ((0, 0), (0, 256 - matrix.shape[1])))


def tables():
    one, two, three = depth_operators()
    depth = np.zeros((2, NZ, 256))
    for f in range(2):
        depth[f, :, 64 * f : 64 * f + 64] = two.T
        depth[f, :, 128 + 32 * f : 160 + 32 * f] = three.T
    own = [ops[0] for ops in OPS]
    up = [ops[1] for ops in OPS]
    down = [ops[2] for ops in OPS]
    sent = [np.concatenate([p, q]) for p, q in zip(up, down)]
    spread2 = np.zeros((2, 64, 2, NZ))
    spread3 = np.zeros((4, 32, 2, NZ))
    for f in range(2):
        for i in range(64):
            spread2[f, i, f, 2 * i] = 1
        for i in range(32):
            spread3[f, i, f, 4 * i] = 1
    groups = [
        {"ya": batched(np.concatenate([sent[0], own[1], sent[1], own[2], sent[2]]))},
        {
            "e2": batched(sent[1]),
            "n2": wide(blocks(own[1], 6)),
            "c2": wide(corner_matrix(up[1], down[1], 4, 16)),
            "e3": batched(sent[2]),
            "n3": wide(blocks(own[2], 7)),
            "c3": wide(corner_matrix(up[2], down[2], 4, 16)),
            "c1": corner_matrix(up[0], down[0], 2, 8),
            "z1": one.T,
            "z23": depth.reshape(256, 256),
        },
        {"o2": batched(own[1]), "o3": batched(own[2]), "x1": blocks(own[0], 4)},
        {"m2": gain_matrix(1), "m3": gain_matrix(2)},
    ]
    packed, where = [], {}
    for group, pairs in enumerate(groups):
        arrays = []

        def put(name, array):
            extra = -array.shape[0] % 16
            where[name] = (group, sum(len(other) for other in arrays), array.shape[0] + extra)
            arrays.append(np.pad(array, ((0, extra), (0, 0))))

        for name, matrix in pairs.items():
            high, low = halves(matrix)
            if matrix.shape[1] == 128:
                put(name, np.concatenate([high, low], 1))
            else:
                put(name + "h", high)
                put(name + "l", low)
        if group == 2:
            high, low = halves(blocks(own[0], 2))
            put("u1", wide(np.concatenate([high, high, low], 1)))
        if group == 3:
            put("p2", np.asarray(spread2.reshape(128, 256), jnp.bfloat16))
            put("p3", np.asarray(spread3.reshape(128, 256), jnp.bfloat16))
        packed.append(np.concatenate(arrays))
    return packed, where


TABLES, WHERE = tables()


def split(value):
    high = value.astype(jnp.bfloat16)
    return high, (value - high.astype(jnp.float32)).astype(jnp.bfloat16)


def dot(a, b):
    return jnp.dot(a, b, preferred_element_type=jnp.float32)


def column(gain, first):
    row = lax.broadcasted_iota(jnp.int32, (8, NZ), 0)
    out = jnp.zeros((8, NZ), jnp.float32)
    for i in range(8):
        if abs(gain[first + i]) > 1e-13:
            out = jnp.where(row == i, jnp.float32(gain[first + i]), out)
    return out


def lift_own(lines):
    pairs = N // 2
    even = lines[0::2]
    odd = lines[1::2]
    zero = jnp.zeros_like(even[0])
    odd = [LIFT_ALPHA * even[0]] + [odd[i] + LIFT_ALPHA * (even[i] + (even[i + 1] if i + 1 < pairs else zero)) for i in range(pairs)]
    even = [LIFT_BETA * odd[0]] + [even[i] + LIFT_BETA * (odd[i] + odd[i + 1]) for i in range(pairs)] + [LIFT_BETA * odd[pairs]]
    odd = [odd[i] + LIFT_GAMMA * (even[i] + even[i + 1]) for i in range(pairs + 1)]
    out = []
    for i in range(pairs):
        out.append((even[i + 1] + LIFT_DELTA * (odd[i] + odd[i + 1])) * (1.0 / LIFT_KAPPA))
        out.append(odd[i + 1] * LIFT_KAPPA)
    return out


def both_of(part, name):
    if name in WHERE:
        return part(name)[:, :128], part(name)[:, 128:]
    return part(name + "h"), part(name + "l")


def reader(*refs):
    def part(name):
        group, at, rows = WHERE[name]
        return refs[group][at : at + rows, :]

    def times(name, pair):
        (ah, al), (bh, bl) = both_of(part, name), pair
        return dot(ah, bh) + dot(ah, bl) + dot(al, bh)

    def timed(pair, name):
        (ah, al), (bh, bl) = pair, both_of(part, name)
        return dot(ah, bh) + dot(al, bh) + dot(ah, bl)

    return part, times, timed


def exchange(nx, ny, v0_ref, v1_ref, table0_ref, table1_ref, table2_ref, table3_ref, own1, got_edge, got_corner, level2, level3, table3, fields, table0, table1, table2, rawh, rawl, states1, states2, states3, lines, send_side, got_side, send_edge, send_corner, relays, in_sem, send_sem, recv_sem):
    ix, iy = lax.axis_index("dx"), lax.axis_index("dy")
    right, left = lax.rem(ix + 1, nx), lax.rem(ix + nx - 1, nx)
    above, below = lax.rem(iy + 1, ny), lax.rem(iy + ny - 1, ny)
    edge_to = [(right, iy), (left, iy), (ix, above), (ix, below)]
    corner_to = [(right, above), (right, below), (left, above), (left, below)]


    def rank(tx, ty):
        return 3 * tx + 2 * ty + 20 * lax.div(2 * ty, ny)

    earlier = [rank(tx, ty) < rank(ix, iy) for tx, ty in corner_to]
    barrier = pltpu.get_barrier_semaphore()
    for there, first in zip(corner_to, earlier):

        @pl.when(jnp.logical_not(first))
        def _():
            pl.semaphore_signal(barrier, inc=1, device_id=there, device_id_type=MESH)

    first_y, last_y = iy == 0, iy == ny - 1
    relayed = [jnp.logical_not(earlier[c] | first_y if c % 2 else earlier[c]) for c in range(4)]
    for k in (3, 1, 0):
        pl.semaphore_signal(barrier, inc=1, device_id=edge_to[k], device_id_type=MESH)

    @pl.when(jnp.logical_not(last_y))
    def _():
        pl.semaphore_signal(barrier, inc=1, device_id=edge_to[2], device_id_type=MESH)

    loads = []
    for i, (source, target) in enumerate(((table0_ref, table0), (v0_ref, fields.at[0]), (v1_ref, fields.at[1]), (table1_ref, table1), (table2_ref, table2), (table3_ref, table3))):
        loads.append(pltpu.make_async_copy(source, target, in_sem.at[i]))
        loads[-1].start()
    part, times, timed = reader(table0, table1, table2)

    def copy_to(at, source, target, there):
        return pltpu.make_async_remote_copy(src_ref=source, dst_ref=target, send_sem=send_sem.at[at], recv_sem=recv_sem.at[at], device_id=there, device_id_type=MESH)

    for load in loads[:3]:
        load.wait()
    for f in range(2):
        for j in range(2):
            at = slice(64 * f + 32 * j, 64 * f + 32 * j + 32)
            send_side[0, at, :] = sum(float(OPS[0][1][j, 28 + i]) * fields[f, 28 + i] for i in range(4))
            send_side[1, at, :] = sum(float(OPS[0][2][j, i]) * fields[f, i] for i in range(3))
    for b in range(4):
        here = slice(8 * b, 8 * b + 8)
        raw = split(jnp.concatenate([fields[f, here].reshape(256, NZ) for f in range(2)], 1))
        rawh[256 * b : 256 * b + 256, :], rawl[256 * b : 256 * b + 256, :] = raw
        value = times("ya", raw).reshape(42, 8, 256)
        states1[:, here, :] = value[:4]
        states2[:, here, :] = value[4:26]
        states3[:, here, :] = value[26:41]
    for k in range(2):
        for f in range(2):
            send_side[2 + k, 64 * f : 64 * f + 64, :] = states1[2 * k : 2 * k + 2, :, 128 * f : 128 * f + 128].reshape(64, NZ)
    loads[3].wait()

    def relay(below):
        for k in range(2):
            pl.semaphore_signal(relays.at[2 - 2 * k + below], inc=1, device_id=edge_to[k], device_id_type=MESH)

    pl.semaphore_wait(barrier, 4 - first_y.astype(jnp.int32) + sum(first.astype(jnp.int32) for first in earlier))

    @pl.when(last_y)
    def _():
        pl.semaphore_signal(relays.at[4], inc=1, device_id=edge_to[2], device_id_type=MESH)

    relay(0)
    pl.when(jnp.logical_not(first_y))(lambda: relay(1))
    sides = [copy_to(8 + k, send_side.at[k], got_side.at[k], edge_to[k]) for k in range(4)]
    for k in range(3):
        sides[k].start()
    pl.when(jnp.logical_not(first_y))(sides[3].start)

    value = [times("e2", split(states2[8 * c : 8 * c + 8].reshape(256, 256))) for c in range(2)]
    rows2 = [value[c][8 * j : 8 * j + 8] for j in range(6) for c in range(2)]
    lines2 = jnp.concatenate([states2[16:22].reshape(192, 256), jnp.zeros((64, 256), jnp.float32)], 0)
    lines2 = split(lines2)
    rows2 += [times("n2", lines2), times("c2", lines2)]
    rows3 = [times("e3", split(states3[0:8].reshape(256, 256)))[:56]]
    lines3 = jnp.concatenate([states3[8:15].reshape(224, 256), jnp.zeros((32, 256), jnp.float32)], 0)
    lines3 = split(lines3)
    rows3 += [times("n3", lines3)[:56], times("c3", lines3)]
    corners1 = times("c1", split(states1[...].reshape(128, 256)))
    zh, zl = both_of(part, "z23")

    def deep(value, half):
        high, low = split(value)
        at = slice(128 * half, 128 * half + 128)
        return dot(high, zh[:, at]) + dot(low, zh[:, at]) + dot(high, zl[:, at])

    value = deep(jnp.concatenate(rows2, 0), 0)
    for k in range(2):
        send_edge[k, 0:48, :] = value[48 * k : 48 * k + 48]
        send_edge[2 + k, 0:48, :] = value[96 + 48 * k : 144 + 48 * k]
    for c in range(4):
        send_corner[c, 16:32, :] = value[192 + 16 * c : 208 + 16 * c]
    value = deep(jnp.concatenate(rows3, 0), 1)
    for k, first in enumerate((0, 32)):
        for axis in range(2):
            count = 32 - 8 * k
            at = 56 * axis + first
            send_edge[2 * axis + k, 48 : 48 + count, :] = value[at : at + count]
    send_edge[1, 72:80, :] = jnp.zeros((8, NZ), jnp.float32)
    send_edge[3, 72:80, :] = jnp.zeros((8, NZ), jnp.float32)
    for c in range(4):
        send_corner[c, 32:48, :] = value[112 + 16 * c : 128 + 16 * c]
    value = timed(split(jnp.concatenate([corners1[:, :128], corners1[:, 128:]], 0)), "z1")
    for c in range(4):
        for f in range(2):
            send_corner[c, 8 * f : 8 * f + 8, :] = value[32 * f + 8 * c : 32 * f + 8 * c + 8]
    copies = [pltpu.make_async_remote_copy(src_ref=send_corner.at[c], dst_ref=got_corner.at[c], send_sem=send_sem.at[c], recv_sem=recv_sem.at[c], device_id=corner_to[c], device_id_type=MESH) for c in range(4)]
    for c in range(4):
        pl.when(earlier[c])(copies[c].start)
    copies += [copy_to(4 + k, send_edge.at[k], got_edge.at[k], edge_to[k]) for k in range(4)]
    for k in range(3):
        copies[4 + k].start()
    pl.when(jnp.logical_not(first_y))(copies[7].start)

    loads[4].wait()
    value = [times("o2", split(states2[8 * c : 8 * c + 8].reshape(256, 256))) for c in range(2)]
    value = deep(jnp.concatenate([value[c][8 * x : 8 * x + 8] for x in range(16) for c in range(2)], 0), 0)
    level2[...] = value
    level3[...] = deep(times("o3", split(states3[0:8].reshape(256, 256))), 1)
    def wait_and_send(c):
        pl.semaphore_wait(relays.at[c], 1)
        copies[c].start()

    for c in (0, 1):
        pl.when(relayed[c])(lambda: wait_and_send(c))

    @pl.when(first_y)
    def _():
        pl.semaphore_wait(relays.at[4], 1)
        relay(1)
        copies[7].start()
        sides[3].start()
        copies[1].start()
        copies[3].start()

    for c in (2, 3):
        pl.when(relayed[c])(lambda: wait_and_send(c))

    own = part("u1")[:, :192]
    for b in range(4):
        rows = slice(256 * b, 256 * b + 256)
        high, low = rawh[rows, :], rawl[rows, :]
        high, low = split(jnp.concatenate([timed((high[:, at : at + 128], low[:, at : at + 128]), "z1") for at in (0, 128)], 1))
        for p in range(4):
            at = slice(64 * p, 64 * p + 64)
            lines[4 * b + p] = dot(own, jnp.concatenate([high[at], low[at], high[at]], 0))
    for f in range(2):
        for t in range(4):
            value = lift_own([lines[i // 2, 32 * (i % 2) + 8 * t : 32 * (i % 2) + 8 * t + 8, 128 * f : 128 * f + 128] for i in range(N)])
            for i in range(N):
                own1[f, i, 8 * t : 8 * t + 8, :] = value[i]

    for copy in sides:
        copy.wait()
    gains = (OPS[0][3], OPS[0][4])
    both = []
    for axis in range(2):
        value = [got_side[2 * axis + k, 64 * f : 64 * f + 64, :] for f in range(2) for k in range(2)]
        value = jnp.concatenate([jnp.concatenate(value[:2], 0), jnp.concatenate(value[2:], 0)], 1)
        value = times("x1", split(value))
        both.append(timed(split(jnp.concatenate([value[:, :128], value[:, 128:]], 0)), "z1"))
    got_side[0], got_side[1] = both[1][:128], both[1][128:]
    for f in range(2):
        for k, xs in enumerate(((0, 1, 2), (28, 29, 30, 31))):
            for x in xs:
                own1[f, x] += sum(float(gains[k][x, j]) * both[0][128 * f + 64 * k + 32 * j : 128 * f + 64 * k + 32 * j + 32] for j in range(2))
        for k in range(2):
            cols = [column(gains[k][:, j], 24 * k) for j in range(2)]
            for x in range(N):
                own1[f, x, 24 * k : 24 * k + 8, :] += sum(cols[j] * got_side[f, 64 * k + 32 * j + x : 64 * k + 32 * j + x + 1, :] for j in range(2))

    loads[5].wait()
    for c in range(4):
        pl.when(jnp.logical_not(relayed[c]))(lambda: pl.semaphore_wait(relays.at[c], 1))
    for copy in copies:
        copy.wait()


def finish(own1, got_edge, got_corner, level2, level3, table3, out0_ref, out1_ref, even, odd, out_sem):
    part, times, _ = reader(None, None, None, table3)
    outs = (out0_ref, out1_ref)
    stores = []

    def store(at, source, target):
        stores.append(pltpu.make_async_copy(source, target, out_sem.at[at]))
        stores[-1].start()

    for f in range(2):
        store(f, own1.at[f, pl.ds(1, 13), 1], outs[f].at[pl.ds(1, 13), 1])

    parts2 = [got_edge[k, 0:48, :] for k in range(4)] + [got_corner[c, 16:32, :] for c in range(4)]
    value2 = times("m2", split(jnp.concatenate(parts2, 0))) + level2[...]
    parts3 = [got_edge[k, 48 : 80 - 8 * (k % 2), :] for k in range(4)] + [got_corner[c, 32:48, :] for c in range(4)]
    parts3.append(jnp.zeros((80, NZ), jnp.float32))
    value3 = times("m3", split(jnp.concatenate(parts3, 0))) + level3[...]
    high, low = split(value2)
    value2 = dot(high, part("p2")) + dot(low, part("p2"))
    high, low = split(value3)
    value3 = dot(high, part("p3")) + dot(low, part("p3"))

    gains = (OPS[0][3], OPS[0][4])
    lane = lax.broadcasted_iota(jnp.int32, (16, NZ), 1)
    cols = [[column(gains[k][:, j], 24 * k) for j in range(2)] for k in range(2)]
    for f in range(2):

        def cornered(x):
            value = [own1[f, x // 2, x % 2, 8 * t : 8 * t + 8, :] for t in range(4)]
            for side, xs in enumerate(((0, 1, 2), (28, 29, 30, 31))):
                if x in xs:
                    for k in range(2):
                        for j in range(2):
                            row = sum(float(gains[side][x, i]) * got_corner[2 * side + k, 8 * f + 2 * j + i : 8 * f + 2 * j + i + 1, :] for i in range(2))
                            value[3 * k] += cols[k][j] * row
            return jnp.concatenate(value, 0)

        for i, x in enumerate((1, 29, 31)):
            odd[f, i] = cornered(x)
        store(2 + f, odd.at[f, 0], outs[f].at[0, 1])
        store(4 + f, odd.at[f, pl.ds(1, 2)], outs[f].at[pl.ds(14, 2), 1])
    for f in range(2):
        for p in range(16):
            even[f, p] = cornered(2 * p)
            cells = even[f, p, pl.ds(0, 16, stride=2), :]
            even[f, p, pl.ds(0, 16, stride=2), :] = jnp.where(lane % 2 == 0, value2[16 * p : 16 * p + 16, 128 * f : 128 * f + 128], cells)
            if p % 2 == 0:
                cells = even[f, p, pl.ds(0, 8, stride=4), :]
                even[f, p, pl.ds(0, 8, stride=4), :] = jnp.where(lane[:8] % 4 == 0, value3[4 * p : 4 * p + 8, 128 * f : 128 * f + 128], cells)
            if p % 8 == 7:
                here = pl.ds(p - 7, 8)
                store(6 + 2 * f + p // 8, even.at[f, here], outs[f].at[here, 0])
    for copy in stores:
        copy.wait()


def solution(mesh):
    nx, ny = mesh.shape["dx"], mesh.shape["dy"]
    f32, bf16 = jnp.float32, jnp.bfloat16

    def body(volume_fraction, vorticity):
        inputs = [volume_fraction, vorticity] + [jnp.asarray(table) for table in TABLES]
        inputs = [pltpu.with_memory_space_constraint(value, pltpu.HBM) for value in inputs]
        passed = (
            pltpu.VMEM((2, N, N, NZ), f32),
            pltpu.VMEM((4, 80, NZ), f32),
            pltpu.VMEM((4, 48, NZ), f32),
            pltpu.VMEM((256, NZ), f32),
            pltpu.VMEM((64, NZ), f32),
            pltpu.VMEM(TABLES[3].shape, bf16),
        )
        middle = pl.pallas_call(
            lambda *refs: exchange(nx, ny, *refs),
            out_shape=passed,
            in_specs=[pl.BlockSpec(memory_space=pltpu.HBM)] * 6,
            out_specs=(pl.BlockSpec(memory_space=pltpu.VMEM),) * 6,
            scratch_shapes=[
                pltpu.VMEM((2, N, N, NZ), f32),
                pltpu.VMEM(TABLES[0].shape, bf16),
                pltpu.VMEM(TABLES[1].shape, bf16),
                pltpu.VMEM(TABLES[2].shape, bf16),
                pltpu.VMEM((1024, 256), bf16),
                pltpu.VMEM((1024, 256), bf16),
                pltpu.VMEM((4, N, 256), f32),
                pltpu.VMEM((22, N, 256), f32),
                pltpu.VMEM((15, N, 256), f32),
                pltpu.VMEM((16, 64, 256), f32),
                pltpu.VMEM((4, 128, NZ), f32),
                pltpu.VMEM((4, 128, NZ), f32),
                pltpu.VMEM((4, 80, NZ), f32),
                pltpu.VMEM((4, 48, NZ), f32),
                pltpu.SemaphoreType.REGULAR((5,)),
                pltpu.SemaphoreType.DMA((6,)),
                pltpu.SemaphoreType.DMA((12,)),
                pltpu.SemaphoreType.DMA((12,)),
            ],
            compiler_params=pltpu.CompilerParams(
                collective_id=0, has_side_effects=True, vmem_limit_bytes=32 * 1024 * 1024
            ),
        )(*inputs)
        middle = [middle[0].reshape(2, 16, 2, N, NZ)] + list(middle[1:])
        middle = [pltpu.with_memory_space_constraint(value, pltpu.VMEM) for value in middle]
        block = pltpu.HBM((16, 2, N, NZ), f32)
        outs = pl.pallas_call(
            finish,
            out_shape=(block, block),
            in_specs=[pl.BlockSpec(memory_space=pltpu.VMEM)] * 6,
            out_specs=(pl.BlockSpec(memory_space=pltpu.HBM),) * 2,
            scratch_shapes=[
                pltpu.VMEM((2, 16, N, NZ), f32),
                pltpu.VMEM((2, 3, N, NZ), f32),
                pltpu.SemaphoreType.DMA((10,)),
            ],
            compiler_params=pltpu.CompilerParams(vmem_limit_bytes=32 * 1024 * 1024),
        )(*middle)
        return tuple(out.reshape(N, N, NZ) for out in outs)

    placed = P("dx", "dy", None)
    return jax.shard_map(
        body, mesh=mesh, in_specs=(placed, placed), out_specs=(placed, placed), check_vma=False
    )
```

time: 16.3 us -> 15.3 us (0.939); the launches traced: 16 us -> 15.2 us
  Pallas kernels: 15.3 us -> 14.6 us
    pallas_call x1, Pallas kernels: 13.8 us -> 13.2 us  [body(): pl.pallas_call(lambda *refs: exchange(nx, ny, *refs), out_shape=passed, i...]
where the time goes in v3:
time: 15.3 us; the launch traced here: 15.2 us
  Pallas kernels  14.6 us (95%)
  between operations  0.64 us (4%)
    pallas_call x1, Pallas kernels, body(): pl.pallas_call(lambda *refs: exchange(nx, ny, *refs), out_shape=passed, i...  13.2 us
    pallas_call x1, Pallas kernels, body(): pl.pallas_call(finish, out_shape=(block, block), in_specs=[pl.BlockSpec(m...  1.37 us

profile of v3, /device:TPU:0, one launch (start us, length us, event | category | flops | bytes accessed | tf_op | source)
XLA Modules:
  0.0 15.2 jit_solution(1639536631530611772)
XLA Ops:
  0.6 13.2 %shard_map.77 = (f32[2,32,32,128]{3,2,1,0:T(8,128)S(1)}, f32[4,80,128]{2,1,0:T(8,128)S(1)}, f32[4,48,128]{2,1,0:T(8,128)S(1)}, f32[256,128]{1,0:T(8,128)S(1)}, f...) custom-call(f32[32,32,128]{2,1,0:T(8,128)} %refs_0_.1, f32[32,32,128]{2,1,0:T(8,128)} %refs_1_.1, ...), custom_call_target="tpu_custom_call" | custom-call | tf_op jit(solution)/shard_map/pallas_call | solution.py:490
  13.8 1.4 %shard_map.78 = (f32[16,2,32,128]{3,2,1,0:T(8,128)}, f32[16,2,32,128]{3,2,1,0:T(8,128)}) custom-call(f32[2,16,2,32,128]{4,3,2,1,0:T(8,128)S(1)} %bitcast.3, f32[4,80,128]{2,1,0:T(8,128)S(1)} %get-tuple-element.11.got_edge, f32[4,48,128]{2,1,0:T(8,128)S(1)} %get-tuple-element.12.got_corner, f32[256,128]{1,0:T(8,128)S(1)} %get-tuple-element.13.level2, ...), custom_call_target="tpu_custom_call" | custom-call | tf_op jit(solution)/shard_map/pallas_call | solution.py:522

commit v4 on v3

--- a/solution.py
+++ b/solution.py
@@ -91,6 +91,8 @@
         for jy in range(len(sent[sy])):
             for jx, line in enumerate(sent[sx]):
                 out[corner, stride * jy + jx, sy * len(up) + jy] = line
+        if rows == 8:
+            out[corner, 4:] = out[corner, :4]
     return out.reshape(4 * rows, total * N)
 
 
@@ -98,11 +100,19 @@
     gains = OPS[level][3:]
     size = N >> level
     eye = np.eye(size)
+    if level == 2:
+        gains = [np.pad(gain, ((0, 0), (0, 4 - gain.shape[1]))) for gain in gains]
     parts = [np.einsum("xj,yv->xyjv", gain, eye).reshape(size * size, -1) for gain in gains]
     parts += [np.einsum("yj,xv->xyjv", gain, eye).reshape(size * size, -1) for gain in gains]
     four = [np.pad(gain, ((0, 0), (0, 4 - gain.shape[1]))) for gain in gains]
     for corner in range(4):
         parts.append(np.einsum("xi,yj->xyji", four[corner // 2], four[corner % 2]).reshape(size * size, 16))
+    if level == 2:
+        for i, width in enumerate([8] * 4 + [1] * 4):
+            states = parts[i].reshape(size * size, -1, 2, width)
+            parts[i] = np.concatenate([states[:, :, half].reshape(size * size, -1) for half in range(2)])
+        out = np.concatenate(parts, 1)
+        return np.pad(out, ((0, 0), (0, 128 - out.shape[1])))
     return wide(np.concatenate(parts, 1))
 
 
@@ -121,7 +131,8 @@
     depth = np.zeros((2, NZ, 256))
     for f in range(2):
         depth[f, :, 64 * f : 64 * f + 64] = two.T
-        depth[f, :, 128 + 32 * f : 160 + 32 * f] = three.T
+        for half in (128, 192):
+            depth[f, :, half + 32 * f : half + 32 * f + 32] = three.T
     own = [ops[0] for ops in OPS]
     up = [ops[1] for ops in OPS]
     down = [ops[2] for ops in OPS]
@@ -132,19 +143,19 @@
         for i in range(64):
             spread2[f, i, f, 2 * i] = 1
         for i in range(32):
-            spread3[f, i, f, 4 * i] = 1
+            spread3[f, i, f, 4 * i] = spread3[2 + f, i, f, 4 * i] = 1
     groups = [
         {"ya": batched(np.concatenate([sent[0], own[1], sent[1], own[2], sent[2]]))},
         {
-            "e2": batched(sent[1]),
-            "n2": wide(blocks(own[1], 6)),
-            "c2": wide(corner_matrix(up[1], down[1], 4, 16)),
-            "e3": batched(sent[2]),
-            "n3": wide(blocks(own[2], 7)),
-            "c3": wide(corner_matrix(up[2], down[2], 4, 16)),
             "c1": corner_matrix(up[0], down[0], 2, 8),
+            "c23": np.concatenate([wide(corner_matrix(up[1], down[1], 4, 16)), wide(corner_matrix(up[2], down[2], 4, 16))]),
             "z1": one.T,
             "z23": depth.reshape(256, 256),
+        },
+        {
+            "e2": batched(sent[1]),
+            "e3": batched(sent[2]),
+            "n23": np.concatenate([wide(blocks(own[1], 6)), wide(blocks(own[2], 7))]),
         },
         {"o2": batched(own[1]), "o3": batched(own[2]), "x1": blocks(own[0], 4)},
         {"m2": gain_matrix(1), "m3": gain_matrix(2)},
@@ -165,10 +176,10 @@
             else:
                 put(name + "h", high)
                 put(name + "l", low)
-        if group == 2:
+        if group == 3:
             high, low = halves(blocks(own[0], 2))
             put("u1", wide(np.concatenate([high, high, low], 1)))
-        if group == 3:
+        if group == 4:
             put("p2", np.asarray(spread2.reshape(128, 256), jnp.bfloat16))
             put("p3", np.asarray(spread3.reshape(128, 256), jnp.bfloat16))
         packed.append(np.concatenate(arrays))
@@ -224,16 +235,27 @@
 
     def times(name, pair):
         (ah, al), (bh, bl) = both_of(part, name), pair
-        return dot(ah, bh) + dot(ah, bl) + dot(al, bh)
+        return dot(jnp.concatenate([ah, ah, al], 1), jnp.concatenate([bh, bl, bh], 0))
 
     def timed(pair, name):
         (ah, al), (bh, bl) = pair, both_of(part, name)
-        return dot(ah, bh) + dot(al, bh) + dot(ah, bl)
+        return dot(jnp.concatenate([ah, al, ah], 1), jnp.concatenate([bh, bh, bl], 0))
 
     return part, times, timed
 
 
-def exchange(nx, ny, v0_ref, v1_ref, table0_ref, table1_ref, table2_ref, table3_ref, own1, got_edge, got_corner, level2, level3, table3, fields, table0, table1, table2, rawh, rawl, states1, states2, states3, lines, send_side, got_side, send_edge, send_corner, relays, in_sem, send_sem, recv_sem):
+def exchange(nx, ny, v0_ref, v1_ref, table0_ref, table1_ref, table2_ref, table3_ref, table4_ref, own1, got_edge, got_corner, level2, level3, table4, fields, table0, table1, table2, table3, rawh, rawl, states1, states2, states3, lines, send_side, got_side, send_edge, send_corner, relays, in_sem, send_sem, recv_sem):
+    loads = []
+
+    def load(source, target):
+        loads.append(pltpu.make_async_copy(source, target, in_sem.at[len(loads)]))
+        loads[-1].start()
+
+    load(table0_ref, table0)
+    for b in range(2):
+        for f, ref in enumerate((v0_ref, v1_ref)):
+            load(ref.at[pl.ds(16 * b, 16)], fields.at[f, pl.ds(16 * b, 16)])
+    load(table1_ref, table1)
     ix, iy = lax.axis_index("dx"), lax.axis_index("dy")
     right, left = lax.rem(ix + 1, nx), lax.rem(ix + nx - 1, nx)
     above, below = lax.rem(iy + 1, ny), lax.rem(iy + ny - 1, ny)
@@ -252,130 +274,133 @@
         def _():
             pl.semaphore_signal(barrier, inc=1, device_id=there, device_id_type=MESH)
 
-    first_y, last_y = iy == 0, iy == ny - 1
-    relayed = [jnp.logical_not(earlier[c] | first_y if c % 2 else earlier[c]) for c in range(4)]
-    for k in (3, 1, 0):
-        pl.semaphore_signal(barrier, inc=1, device_id=edge_to[k], device_id_type=MESH)
-
-    @pl.when(jnp.logical_not(last_y))
-    def _():
-        pl.semaphore_signal(barrier, inc=1, device_id=edge_to[2], device_id_type=MESH)
-
-    loads = []
-    for i, (source, target) in enumerate(((table0_ref, table0), (v0_ref, fields.at[0]), (v1_ref, fields.at[1]), (table1_ref, table1), (table2_ref, table2), (table3_ref, table3))):
-        loads.append(pltpu.make_async_copy(source, target, in_sem.at[i]))
-        loads[-1].start()
-    part, times, timed = reader(table0, table1, table2)
+    first_x, last_x, first_y, last_y = ix == 0, ix == nx - 1, iy == 0, iy == ny - 1
+    inner_x, inner_y = jnp.logical_not(first_x), jnp.logical_not(first_y)
+    relayed = [jnp.logical_not(e) for e in (earlier[0], earlier[1] | first_y, earlier[2], earlier[3] | first_y)]
+    for k, say in ((3, None), (1, None), (2, jnp.logical_not(last_y)), (0, jnp.logical_not(last_x))):
+
+        def signal():
+            pl.semaphore_signal(barrier, inc=1, device_id=edge_to[k], device_id_type=MESH)
+
+        signal() if say is None else pl.when(say)(signal)
+
+    part, times, timed = reader(table0, table1, table2, table3)
 
     def copy_to(at, source, target, there):
         return pltpu.make_async_remote_copy(src_ref=source, dst_ref=target, send_sem=send_sem.at[at], recv_sem=recv_sem.at[at], device_id=there, device_id_type=MESH)
 
-    for load in loads[:3]:
-        load.wait()
-    for f in range(2):
-        for j in range(2):
-            at = slice(64 * f + 32 * j, 64 * f + 32 * j + 32)
-            send_side[0, at, :] = sum(float(OPS[0][1][j, 28 + i]) * fields[f, 28 + i] for i in range(4))
-            send_side[1, at, :] = sum(float(OPS[0][2][j, i]) * fields[f, i] for i in range(3))
+    loads[0].wait()
     for b in range(4):
         here = slice(8 * b, 8 * b + 8)
+        if b % 2 == 0:
+            loads[2 * (b // 2) + 1].wait()
+            loads[2 * (b // 2) + 2].wait()
         raw = split(jnp.concatenate([fields[f, here].reshape(256, NZ) for f in range(2)], 1))
         rawh[256 * b : 256 * b + 256, :], rawl[256 * b : 256 * b + 256, :] = raw
         value = times("ya", raw).reshape(42, 8, 256)
         states1[:, here, :] = value[:4]
         states2[:, here, :] = value[4:26]
         states3[:, here, :] = value[26:41]
+    for f in range(2):
+        for j in range(2):
+            at = slice(64 * f + 32 * j, 64 * f + 32 * j + 32)
+            send_side[0, at, :] = sum(float(OPS[0][1][j, 28 + i]) * fields[f, 28 + i] for i in range(4))
+            send_side[1, at, :] = sum(float(OPS[0][2][j, i]) * fields[f, i] for i in range(3))
     for k in range(2):
         for f in range(2):
             send_side[2 + k, 64 * f : 64 * f + 64, :] = states1[2 * k : 2 * k + 2, :, 128 * f : 128 * f + 128].reshape(64, NZ)
-    loads[3].wait()
-
-    def relay(below):
-        for k in range(2):
-            pl.semaphore_signal(relays.at[2 - 2 * k + below], inc=1, device_id=edge_to[k], device_id_type=MESH)
-
-    pl.semaphore_wait(barrier, 4 - first_y.astype(jnp.int32) + sum(first.astype(jnp.int32) for first in earlier))
-
-    @pl.when(last_y)
+    for source, target in ((table2_ref, table2), (table3_ref, table3), (table4_ref, table4)):
+        load(source, target)
+    def answer(at, k):
+        pl.semaphore_signal(relays.at[at], inc=1, device_id=edge_to[k], device_id_type=MESH)
+
+    def relay(below, k):
+        answer(2 - 2 * k + below, k)
+
+    pl.semaphore_wait(barrier, 2 + inner_x.astype(jnp.int32) + inner_y.astype(jnp.int32) + sum(first.astype(jnp.int32) for first in earlier))
+    pl.when(last_y)(lambda: answer(4, 2))
+    pl.when(last_x)(lambda: answer(5, 0))
+
+    @pl.when(last_x & last_y)
     def _():
-        pl.semaphore_signal(relays.at[4], inc=1, device_id=edge_to[2], device_id_type=MESH)
-
-    relay(0)
-    pl.when(jnp.logical_not(first_y))(lambda: relay(1))
+        pl.semaphore_signal(relays.at[6], inc=1, device_id=corner_to[0], device_id_type=MESH)
+
+    relay(0, 0)
+    pl.when(inner_x)(lambda: relay(0, 1))
+    pl.when(inner_y)(lambda: relay(1, 0))
+    pl.when(inner_x & inner_y)(lambda: relay(1, 1))
     sides = [copy_to(8 + k, send_side.at[k], got_side.at[k], edge_to[k]) for k in range(4)]
-    for k in range(3):
-        sides[k].start()
-    pl.when(jnp.logical_not(first_y))(sides[3].start)
-
+
+    def start_inner(group):
+        group[0].start()
+        group[2].start()
+        pl.when(inner_x)(group[1].start)
+        pl.when(inner_y)(group[3].start)
+
+    start_inner(sides)
+
+    loads[5].wait()
+    zh, zl = both_of(part, "z23")
+
+    def deep(value, half):
+        return deep_of(split(value), half)
+
+    def deep_of(pair, half):
+        high, low = pair
+        at = slice(128 * half, 128 * half + 128)
+        return dot(jnp.concatenate([high, low, high], 1), jnp.concatenate([zh[:, at], zh[:, at], zl[:, at]], 0))
+
+    corners1 = times("c1", split(states1[...].reshape(128, 256)))
+    lines2 = split(states2[16:22].reshape(192, 256))
+    lines3 = split(states3[8:15].reshape(224, 256))
+    deep2 = jnp.concatenate([deep_of(lines2, 0), jnp.zeros((64, NZ), jnp.float32)], 0)
+    deep3 = jnp.concatenate([deep_of(lines3, 1), jnp.zeros((32, NZ), jnp.float32)], 0)
+    both = split(jnp.concatenate([deep2, deep3], 1))
+    corners1 = timed(split(jnp.concatenate([corners1[:, :128], corners1[:, 128:]], 0)), "z1")
+    value = times("c23", both)
+    corners2, corners3 = value[:64, :128], value[64:, 128:]
+    along_y = both
+    row = lax.broadcasted_iota(jnp.int32, (8, NZ), 0)
+    lane = lax.broadcasted_iota(jnp.int32, (8, NZ), 1)
+
+    def beside(value, at, apart, step):
+        if step == 8:
+            return jnp.where(lane < 64, value[at : at + 8], value[at + apart : at + apart + 8])
+        pairs = value[at : at + 16].reshape(8, 2, NZ)
+        return jnp.where(lane < 64, pairs[:, 0], pairs[:, 1])
+
+    for c in range(4):
+        send_corner[c, 0:8, :] = jnp.where(row < 4, corners1[8 * c : 8 * c + 8], corners1[32 + 8 * c : 40 + 8 * c])
+        send_corner[c, 8:24, :] = corners2[16 * c : 16 * c + 16]
+        send_corner[c, 24:32, :] = beside(corners3, 16 * c, 1, 1)
+    copies = [copy_to(c, send_corner.at[c], got_corner.at[c], corner_to[c]) for c in range(4)]
+    for c in range(4):
+        pl.when(earlier[c])(copies[c].start)
+    loads[6].wait()
     value = [times("e2", split(states2[8 * c : 8 * c + 8].reshape(256, 256))) for c in range(2)]
     rows2 = [value[c][8 * j : 8 * j + 8] for j in range(6) for c in range(2)]
-    lines2 = jnp.concatenate([states2[16:22].reshape(192, 256), jnp.zeros((64, 256), jnp.float32)], 0)
-    lines2 = split(lines2)
-    rows2 += [times("n2", lines2), times("c2", lines2)]
-    rows3 = [times("e3", split(states3[0:8].reshape(256, 256)))[:56]]
-    lines3 = jnp.concatenate([states3[8:15].reshape(224, 256), jnp.zeros((32, 256), jnp.float32)], 0)
-    lines3 = split(lines3)
-    rows3 += [times("n3", lines3)[:56], times("c3", lines3)]
-    corners1 = times("c1", split(states1[...].reshape(128, 256)))
-    zh, zl = both_of(part, "z23")
-
-    def deep(value, half):
-        high, low = split(value)
-        at = slice(128 * half, 128 * half + 128)
-        return dot(high, zh[:, at]) + dot(low, zh[:, at]) + dot(high, zl[:, at])
-
+    rows3 = times("e3", split(states3[0:8].reshape(256, 256)))[:56]
+    sides_y = times("n23", along_y)
     value = deep(jnp.concatenate(rows2, 0), 0)
     for k in range(2):
         send_edge[k, 0:48, :] = value[48 * k : 48 * k + 48]
-        send_edge[2 + k, 0:48, :] = value[96 + 48 * k : 144 + 48 * k]
-    for c in range(4):
-        send_corner[c, 16:32, :] = value[192 + 16 * c : 208 + 16 * c]
-    value = deep(jnp.concatenate(rows3, 0), 1)
-    for k, first in enumerate((0, 32)):
-        for axis in range(2):
-            count = 32 - 8 * k
-            at = 56 * axis + first
-            send_edge[2 * axis + k, 48 : 48 + count, :] = value[at : at + count]
-    send_edge[1, 72:80, :] = jnp.zeros((8, NZ), jnp.float32)
-    send_edge[3, 72:80, :] = jnp.zeros((8, NZ), jnp.float32)
-    for c in range(4):
-        send_corner[c, 32:48, :] = value[112 + 16 * c : 128 + 16 * c]
-    value = timed(split(jnp.concatenate([corners1[:, :128], corners1[:, 128:]], 0)), "z1")
-    for c in range(4):
-        for f in range(2):
-            send_corner[c, 8 * f : 8 * f + 8, :] = value[32 * f + 8 * c : 32 * f + 8 * c + 8]
-    copies = [pltpu.make_async_remote_copy(src_ref=send_corner.at[c], dst_ref=got_corner.at[c], send_sem=send_sem.at[c], recv_sem=recv_sem.at[c], device_id=corner_to[c], device_id_type=MESH) for c in range(4)]
-    for c in range(4):
-        pl.when(earlier[c])(copies[c].start)
-    copies += [copy_to(4 + k, send_edge.at[k], got_edge.at[k], edge_to[k]) for k in range(4)]
-    for k in range(3):
-        copies[4 + k].start()
-    pl.when(jnp.logical_not(first_y))(copies[7].start)
-
-    loads[4].wait()
+        send_edge[2 + k, 0:48, :] = sides_y[48 * k : 48 * k + 48, :128]
+    value = jnp.concatenate([deep(rows3, 1), sides_y[96:152, 128:]], 0)
+    for axis in range(2):
+        at = 56 * axis
+        send_edge[2 * axis, 48:56, :] = beside(value, at, 8, 8)
+        send_edge[2 * axis, 56:64, :] = beside(value, at + 16, 8, 8)
+        send_edge[2 * axis + 1, 48:56, :] = beside(value, at + 32, 8, 8)
+        send_edge[2 * axis + 1, 56:64, :] = jnp.where(lane < 64, value[at + 48 : at + 56], 0.0)
+    edges = [copy_to(4 + k, send_edge.at[k], got_edge.at[k], edge_to[k]) for k in range(4)]
+    start_inner(edges)
+
+    loads[7].wait()
     value = [times("o2", split(states2[8 * c : 8 * c + 8].reshape(256, 256))) for c in range(2)]
     value = deep(jnp.concatenate([value[c][8 * x : 8 * x + 8] for x in range(16) for c in range(2)], 0), 0)
     level2[...] = value
-    level3[...] = deep(times("o3", split(states3[0:8].reshape(256, 256))), 1)
-    def wait_and_send(c):
-        pl.semaphore_wait(relays.at[c], 1)
-        copies[c].start()
-
-    for c in (0, 1):
-        pl.when(relayed[c])(lambda: wait_and_send(c))
-
-    @pl.when(first_y)
-    def _():
-        pl.semaphore_wait(relays.at[4], 1)
-        relay(1)
-        copies[7].start()
-        sides[3].start()
-        copies[1].start()
-        copies[3].start()
-
-    for c in (2, 3):
-        pl.when(relayed[c])(lambda: wait_and_send(c))
-
+    value = deep(times("o3", split(states3[0:8].reshape(256, 256))), 1)
+    level3[...] = jnp.where(lax.broadcasted_iota(jnp.int32, (64, NZ), 1) < 64, value, 0.0)
     own = part("u1")[:, :192]
     for b in range(4):
         rows = slice(256 * b, 256 * b + 256)
@@ -389,6 +414,40 @@
             value = lift_own([lines[i // 2, 32 * (i % 2) + 8 * t : 32 * (i % 2) + 8 * t + 8, 128 * f : 128 * f + 128] for i in range(N)])
             for i in range(N):
                 own1[f, i, 8 * t : 8 * t + 8, :] = value[i]
+
+    def wait_and_send(c):
+        pl.semaphore_wait(relays.at[c], 1)
+        copies[c].start()
+
+    for c in (0, 1):
+        pl.when(relayed[c])(lambda: wait_and_send(c))
+
+    @pl.when(first_x)
+    def _():
+        pl.semaphore_wait(relays.at[5], 1)
+        relay(0, 1)
+        pl.when(inner_y)(lambda: relay(1, 1))
+        edges[1].start()
+        sides[1].start()
+
+    pl.when(relayed[2])(lambda: wait_and_send(2))
+
+    @pl.when(first_y)
+    def _():
+        pl.semaphore_wait(relays.at[4], 1)
+        relay(1, 0)
+        relay(1, 1)
+        edges[3].start()
+        sides[3].start()
+        copies[1].start()
+        pl.when(inner_x)(copies[3].start)
+
+    pl.when(relayed[3])(lambda: wait_and_send(3))
+
+    @pl.when(first_x & first_y)
+    def _():
+        pl.semaphore_wait(relays.at[6], 1)
+        copies[3].start()
 
     for copy in sides:
         copy.wait()
@@ -409,15 +468,15 @@
             for x in range(N):
                 own1[f, x, 24 * k : 24 * k + 8, :] += sum(cols[j] * got_side[f, 64 * k + 32 * j + x : 64 * k + 32 * j + x + 1, :] for j in range(2))
 
-    loads[5].wait()
+    loads[8].wait()
     for c in range(4):
         pl.when(jnp.logical_not(relayed[c]))(lambda: pl.semaphore_wait(relays.at[c], 1))
-    for copy in copies:
+    for copy in copies + edges:
         copy.wait()
 
 
-def finish(own1, got_edge, got_corner, level2, level3, table3, out0_ref, out1_ref, even, odd, out_sem):
-    part, times, _ = reader(None, None, None, table3)
+def finish(own1, got_edge, got_corner, level2, level3, table4, out0_ref, out1_ref, even, odd, out_sem):
+    part, times, _ = reader(None, None, None, None, table4)
     outs = (out0_ref, out1_ref)
     stores = []
 
@@ -428,15 +487,16 @@
     for f in range(2):
         store(f, own1.at[f, pl.ds(1, 13), 1], outs[f].at[pl.ds(1, 13), 1])
 
-    parts2 = [got_edge[k, 0:48, :] for k in range(4)] + [got_corner[c, 16:32, :] for c in range(4)]
+    parts2 = [got_edge[k, 0:48, :] for k in range(4)] + [got_corner[c, 8:24, :] for c in range(4)]
     value2 = times("m2", split(jnp.concatenate(parts2, 0))) + level2[...]
-    parts3 = [got_edge[k, 48 : 80 - 8 * (k % 2), :] for k in range(4)] + [got_corner[c, 32:48, :] for c in range(4)]
-    parts3.append(jnp.zeros((80, NZ), jnp.float32))
-    value3 = times("m3", split(jnp.concatenate(parts3, 0))) + level3[...]
+    parts3 = [got_edge[k, 48:64, :] for k in range(4)] + [got_corner[c, 24:32, :] for c in range(4)]
+    parts3.append(jnp.zeros((32, NZ), jnp.float32))
+    value3 = times("m3", split(jnp.concatenate(parts3, 0)))
+    value3 = jnp.where(lax.broadcasted_iota(jnp.int32, (64, NZ), 1) < 64, value3[:64], value3[64:]) + level3[...]
     high, low = split(value2)
-    value2 = dot(high, part("p2")) + dot(low, part("p2"))
+    value2 = dot(jnp.concatenate([high, low], 1), jnp.concatenate([part("p2")] * 2, 0))
     high, low = split(value3)
-    value3 = dot(high, part("p3")) + dot(low, part("p3"))
+    value3 = dot(jnp.concatenate([high, low], 1), jnp.concatenate([part("p3")] * 2, 0))
 
     gains = (OPS[0][3], OPS[0][4])
     lane = lax.broadcasted_iota(jnp.int32, (16, NZ), 1)
@@ -449,7 +509,7 @@
                 if x in xs:
                     for k in range(2):
                         for j in range(2):
-                            row = sum(float(gains[side][x, i]) * got_corner[2 * side + k, 8 * f + 2 * j + i : 8 * f + 2 * j + i + 1, :] for i in range(2))
+                            row = sum(float(gains[side][x, i]) * got_corner[2 * side + k, 4 * f + 2 * j + i : 4 * f + 2 * j + i + 1, :] for i in range(2))
                             value[3 * k] += cols[k][j] * row
             return jnp.concatenate(value, 0)
 
@@ -481,22 +541,23 @@
         inputs = [pltpu.with_memory_space_constraint(value, pltpu.HBM) for value in inputs]
         passed = (
             pltpu.VMEM((2, N, N, NZ), f32),
-            pltpu.VMEM((4, 80, NZ), f32),
-            pltpu.VMEM((4, 48, NZ), f32),
+            pltpu.VMEM((4, 64, NZ), f32),
+            pltpu.VMEM((4, 32, NZ), f32),
             pltpu.VMEM((256, NZ), f32),
             pltpu.VMEM((64, NZ), f32),
-            pltpu.VMEM(TABLES[3].shape, bf16),
+            pltpu.VMEM(TABLES[4].shape, bf16),
         )
         middle = pl.pallas_call(
             lambda *refs: exchange(nx, ny, *refs),
             out_shape=passed,
-            in_specs=[pl.BlockSpec(memory_space=pltpu.HBM)] * 6,
+            in_specs=[pl.BlockSpec(memory_space=pltpu.HBM)] * 7,
             out_specs=(pl.BlockSpec(memory_space=pltpu.VMEM),) * 6,
             scratch_shapes=[
                 pltpu.VMEM((2, N, N, NZ), f32),
                 pltpu.VMEM(TABLES[0].shape, bf16),
                 pltpu.VMEM(TABLES[1].shape, bf16),
                 pltpu.VMEM(TABLES[2].shape, bf16),
+                pltpu.VMEM(TABLES[3].shape, bf16),
                 pltpu.VMEM((1024, 256), bf16),
                 pltpu.VMEM((1024, 256), bf16),
                 pltpu.VMEM((4, N, 256), f32),
@@ -505,10 +566,10 @@
                 pltpu.VMEM((16, 64, 256), f32),
                 pltpu.VMEM((4, 128, NZ), f32),
                 pltpu.VMEM((4, 128, NZ), f32),
-                pltpu.VMEM((4, 80, NZ), f32),
-                pltpu.VMEM((4, 48, NZ), f32),
-                pltpu.SemaphoreType.REGULAR((5,)),
-                pltpu.SemaphoreType.DMA((6,)),
+                pltpu.VMEM((4, 64, NZ), f32),
+                pltpu.VMEM((4, 32, NZ), f32),
+                pltpu.SemaphoreType.REGULAR((7,)),
+                pltpu.SemaphoreType.DMA((13,)),
                 pltpu.SemaphoreType.DMA((12,)),
                 pltpu.SemaphoreType.DMA((12,)),
             ],

time: 15.3 us -> 15.1 us (0.987)
  Pallas kernels: 14.6 us -> 14.3 us
    pallas_call x1, Pallas kernels: 13.2 us -> 13 us  [body(): pl.pallas_call(lambda *refs: exchange(nx, ny, *refs), out_shape=passed, i...]
where the time goes in v4:
time: 15.1 us; the launch traced here: 15 us
  Pallas kernels  14.3 us (95%)
  between operations  0.64 us (4%)
    pallas_call x1, Pallas kernels, body(): pl.pallas_call(lambda *refs: exchange(nx, ny, *refs), out_shape=passed, i...  13 us
    pallas_call x1, Pallas kernels, body(): pl.pallas_call(finish, out_shape=(block, block), in_specs=[pl.BlockSpec(m...  1.3 us

profile of v4, /device:TPU:0, one launch (start us, length us, event | category | flops | bytes accessed | tf_op | source)
XLA Modules:
  0.0 15.0 jit_solution(14687624088794666965)
XLA Ops:
  0.6 13.0 %shard_map.86 = (f32[2,32,32,128]{3,2,1,0:T(8,128)S(1)}, f32[4,64,128]{2,1,0:T(8,128)S(1)}, f32[4,32,128]{2,1,0:T(8,128)S(1)}, f32[256,128]{1,0:T(8,128)S(1)}, f...) custom-call(f32[32,32,128]{2,1,0:T(8,128)} %refs_0_.1, f32[32,32,128]{2,1,0:T(8,128)} %refs_1_.1, ...), custom_call_target="tpu_custom_call" | custom-call | tf_op jit(solution)/shard_map/pallas_call | solution.py:550
  13.7 1.3 %shard_map.87 = (f32[16,2,32,128]{3,2,1,0:T(8,128)}, f32[16,2,32,128]{3,2,1,0:T(8,128)}) custom-call(f32[2,16,2,32,128]{4,3,2,1,0:T(8,128)S(1)} %bitcast.3, f32[4,64,128]{2,1,0:T(8,128)S(1)} %get-tuple-element.11.got_edge, f32[4,32,128]{2,1,0:T(8,128)S(1)} %get-tuple-element.12.got_corner, f32[256,128]{1,0:T(8,128)S(1)} %get-tuple-element.13.level2, ...), custom_call_target="tpu_custom_call" | custom-call | tf_op jit(solution)/shard_map/pallas_call | solution.py:583

commit v5 on v4

--- a/solution.py
+++ b/solution.py
@@ -82,7 +82,7 @@
     return out.reshape(rows * 8, 8 * cols)
 
 
-def corner_matrix(up, down, stride, rows):
+def corner_matrix(up, down, stride, rows, split_lanes=False):
     sent = (up, down)
     total = len(up) + len(down)
     out = np.zeros((4, rows, total, N))
@@ -90,7 +90,8 @@
         sx, sy = corner // 2, corner % 2
         for jy in range(len(sent[sy])):
             for jx, line in enumerate(sent[sx]):
-                out[corner, stride * jy + jx, sy * len(up) + jy] = line
+                at = 8 * (jx % 2) + 2 * jy + jx // 2 if split_lanes else stride * jy + jx
+                out[corner, at, sy * len(up) + jy] = line
         if rows == 8:
             out[corner, 4:] = out[corner, :4]
     return out.reshape(4 * rows, total * N)
@@ -145,14 +146,15 @@
         for i in range(32):
             spread3[f, i, f, 4 * i] = spread3[2 + f, i, f, 4 * i] = 1
     groups = [
-        {"ya": batched(np.concatenate([sent[0], own[1], sent[1], own[2], sent[2]]))},
+        {"ys": batched(np.concatenate(sent))},
         {
             "c1": corner_matrix(up[0], down[0], 2, 8),
-            "c23": np.concatenate([wide(corner_matrix(up[1], down[1], 4, 16)), wide(corner_matrix(up[2], down[2], 4, 16))]),
+            "c23": np.concatenate([wide(corner_matrix(up[1], down[1], 4, 16)), wide(corner_matrix(up[2], down[2], 4, 16, True))]),
             "z1": one.T,
             "z23": depth.reshape(256, 256),
         },
         {
+            "yo": batched(np.concatenate(own[1:])),
             "e2": batched(sent[1]),
             "e3": batched(sent[2]),
             "n23": np.concatenate([wide(blocks(own[1], 6)), wide(blocks(own[2], 7))]),
@@ -171,7 +173,9 @@
 
         for name, matrix in pairs.items():
             high, low = halves(matrix)
-            if matrix.shape[1] == 128:
+            if name == "ys":
+                put(name, np.concatenate([np.pad(half, ((0, 8), (0, 0))) for half in (high, low)]))
+            elif matrix.shape[1] == 128:
                 put(name, np.concatenate([high, low], 1))
             else:
                 put(name + "h", high)
@@ -235,11 +239,13 @@
 
     def times(name, pair):
         (ah, al), (bh, bl) = both_of(part, name), pair
-        return dot(jnp.concatenate([ah, ah, al], 1), jnp.concatenate([bh, bl, bh], 0))
+        value = dot(jnp.concatenate([ah, al], 0), bh)
+        return value[: ah.shape[0]] + value[ah.shape[0] :] + dot(ah, bl)
 
     def timed(pair, name):
         (ah, al), (bh, bl) = pair, both_of(part, name)
-        return dot(jnp.concatenate([ah, al, ah], 1), jnp.concatenate([bh, bh, bl], 0))
+        value = dot(jnp.concatenate([ah, al], 0), bh)
+        return value[: ah.shape[0]] + value[ah.shape[0] :] + dot(ah, bl)
 
     return part, times, timed
 
@@ -297,10 +303,11 @@
             loads[2 * (b // 2) + 2].wait()
         raw = split(jnp.concatenate([fields[f, here].reshape(256, NZ) for f in range(2)], 1))
         rawh[256 * b : 256 * b + 256, :], rawl[256 * b : 256 * b + 256, :] = raw
-        value = times("ya", raw).reshape(42, 8, 256)
+        value = dot(part("ys"), raw[0])
+        value = (value[:144] + value[144:] + dot(part("ys")[:144], raw[1])).reshape(18, 8, 256)
         states1[:, here, :] = value[:4]
-        states2[:, here, :] = value[4:26]
-        states3[:, here, :] = value[26:41]
+        states2[16:22, here, :] = value[4:10]
+        states3[8:15, here, :] = value[10:17]
     for f in range(2):
         for j in range(2):
             at = slice(64 * f + 32 * j, 64 * f + 32 * j + 32)
@@ -348,7 +355,8 @@
     def deep_of(pair, half):
         high, low = pair
         at = slice(128 * half, 128 * half + 128)
-        return dot(jnp.concatenate([high, low, high], 1), jnp.concatenate([zh[:, at], zh[:, at], zl[:, at]], 0))
+        value = dot(jnp.concatenate([high, low], 0), zh[:, at])
+        return value[: high.shape[0]] + value[high.shape[0] :] + dot(high, zl[:, at])
 
     corners1 = times("c1", split(states1[...].reshape(128, 256)))
     lines2 = split(states2[16:22].reshape(192, 256))
@@ -363,20 +371,23 @@
     row = lax.broadcasted_iota(jnp.int32, (8, NZ), 0)
     lane = lax.broadcasted_iota(jnp.int32, (8, NZ), 1)
 
-    def beside(value, at, apart, step):
-        if step == 8:
-            return jnp.where(lane < 64, value[at : at + 8], value[at + apart : at + apart + 8])
-        pairs = value[at : at + 16].reshape(8, 2, NZ)
-        return jnp.where(lane < 64, pairs[:, 0], pairs[:, 1])
+    def beside(value, at):
+        return jnp.where(lane < 64, value[at : at + 8], value[at + 8 : at + 16])
 
     for c in range(4):
         send_corner[c, 0:8, :] = jnp.where(row < 4, corners1[8 * c : 8 * c + 8], corners1[32 + 8 * c : 40 + 8 * c])
         send_corner[c, 8:24, :] = corners2[16 * c : 16 * c + 16]
-        send_corner[c, 24:32, :] = beside(corners3, 16 * c, 1, 1)
+        send_corner[c, 24:32, :] = beside(corners3, 16 * c)
     copies = [copy_to(c, send_corner.at[c], got_corner.at[c], corner_to[c]) for c in range(4)]
     for c in range(4):
         pl.when(earlier[c])(copies[c].start)
     loads[6].wait()
+    for b in range(4):
+        here = slice(8 * b, 8 * b + 8)
+        raw = rawh[256 * b : 256 * b + 256, :], rawl[256 * b : 256 * b + 256, :]
+        value = times("yo", raw).reshape(24, 8, 256)
+        states2[0:16, here, :] = value[:16]
+        states3[0:8, here, :] = value[16:]
     value = [times("e2", split(states2[8 * c : 8 * c + 8].reshape(256, 256))) for c in range(2)]
     rows2 = [value[c][8 * j : 8 * j + 8] for j in range(6) for c in range(2)]
     rows3 = times("e3", split(states3[0:8].reshape(256, 256)))[:56]
@@ -388,9 +399,9 @@
     value = jnp.concatenate([deep(rows3, 1), sides_y[96:152, 128:]], 0)
     for axis in range(2):
         at = 56 * axis
-        send_edge[2 * axis, 48:56, :] = beside(value, at, 8, 8)
-        send_edge[2 * axis, 56:64, :] = beside(value, at + 16, 8, 8)
-        send_edge[2 * axis + 1, 48:56, :] = beside(value, at + 32, 8, 8)
+        send_edge[2 * axis, 48:56, :] = beside(value, at)
+        send_edge[2 * axis, 56:64, :] = beside(value, at + 16)
+        send_edge[2 * axis + 1, 48:56, :] = beside(value, at + 32)
         send_edge[2 * axis + 1, 56:64, :] = jnp.where(lane < 64, value[at + 48 : at + 56], 0.0)
     edges = [copy_to(4 + k, send_edge.at[k], got_edge.at[k], edge_to[k]) for k in range(4)]
     start_inner(edges)

time: 15.1 us -> 14.7 us (0.974)
  Pallas kernels: 14.3 us -> 13.9 us
    pallas_call x1, Pallas kernels: 13 us -> 12.7 us  [body(): pl.pallas_call(lambda *refs: exchange(nx, ny, *refs), out_shape=passed, i...]
where the time goes in v5:
time: 14.7 us; the launch traced here: 14.6 us
  Pallas kernels  13.9 us (95%)
  between operations  0.64 us (4%)
    pallas_call x1, Pallas kernels, body(): pl.pallas_call(lambda *refs: exchange(nx, ny, *refs), out_shape=passed, i...  12.7 us
    pallas_call x1, Pallas kernels, body(): pl.pallas_call(finish, out_shape=(block, block), in_specs=[pl.BlockSpec(m...  1.26 us

profile of v5, /device:TPU:0, one launch (start us, length us, event | category | flops | bytes accessed | tf_op | source)
XLA Modules:
  0.0 14.6 jit_solution(1926350733365097259)
XLA Ops:
  0.6 12.7 %shard_map.86 = (f32[2,32,32,128]{3,2,1,0:T(8,128)S(1)}, f32[4,64,128]{2,1,0:T(8,128)S(1)}, f32[4,32,128]{2,1,0:T(8,128)S(1)}, f32[256,128]{1,0:T(8,128)S(1)}, f...) custom-call(f32[32,32,128]{2,1,0:T(8,128)} %refs_0_.1, f32[32,32,128]{2,1,0:T(8,128)} %refs_1_.1, ...), custom_call_target="tpu_custom_call" | custom-call | tf_op jit(solution)/shard_map/pallas_call | solution.py:561
  13.3 1.3 %shard_map.87 = (f32[16,2,32,128]{3,2,1,0:T(8,128)}, f32[16,2,32,128]{3,2,1,0:T(8,128)}) custom-call(f32[2,16,2,32,128]{4,3,2,1,0:T(8,128)S(1)} %bitcast.3, f32[4,64,128]{2,1,0:T(8,128)S(1)} %get-tuple-element.11.got_edge, f32[4,32,128]{2,1,0:T(8,128)S(1)} %get-tuple-element.12.got_corner, f32[256,128]{1,0:T(8,128)S(1)} %get-tuple-element.13.level2, ...), custom_call_target="tpu_custom_call" | custom-call | tf_op jit(solution)/shard_map/pallas_call | solution.py:594

commit v6 on v5

--- a/solution.py
+++ b/solution.py
@@ -358,14 +358,14 @@
         value = dot(jnp.concatenate([high, low], 0), zh[:, at])
         return value[: high.shape[0]] + value[high.shape[0] :] + dot(high, zl[:, at])
 
-    corners1 = times("c1", split(states1[...].reshape(128, 256)))
     lines2 = split(states2[16:22].reshape(192, 256))
     lines3 = split(states3[8:15].reshape(224, 256))
     deep2 = jnp.concatenate([deep_of(lines2, 0), jnp.zeros((64, NZ), jnp.float32)], 0)
     deep3 = jnp.concatenate([deep_of(lines3, 1), jnp.zeros((32, NZ), jnp.float32)], 0)
     both = split(jnp.concatenate([deep2, deep3], 1))
+    value = times("c23", both)
+    corners1 = times("c1", split(states1[...].reshape(128, 256)))
     corners1 = timed(split(jnp.concatenate([corners1[:, :128], corners1[:, 128:]], 0)), "z1")
-    value = times("c23", both)
     corners2, corners3 = value[:64, :128], value[64:, 128:]
     along_y = both
     row = lax.broadcasted_iota(jnp.int32, (8, NZ), 0)
@@ -482,8 +482,12 @@
     loads[8].wait()
     for c in range(4):
         pl.when(jnp.logical_not(relayed[c]))(lambda: pl.semaphore_wait(relays.at[c], 1))
-    for copy in copies + edges:
+    for copy in edges:
         copy.wait()
+    for copy in copies:
+        copy.wait_send()
+    for c in (3, 2, 1, 0):
+        copies[c].wait_recv()
 
 
 def finish(own1, got_edge, got_corner, level2, level3, table4, out0_ref, out1_ref, even, odd, out_sem):

time: 14.7 us -> 14.7 us (level)
  no operation moved by 1% of the time
where the time goes in v6:
time: 14.7 us; the launch traced here: 14.6 us
  Pallas kernels  13.9 us (95%)
  between operations  0.64 us (4%)
    pallas_call x1, Pallas kernels, body(): pl.pallas_call(lambda *refs: exchange(nx, ny, *refs), out_shape=passed, i...  12.7 us
    pallas_call x1, Pallas kernels, body(): pl.pallas_call(finish, out_shape=(block, block), in_specs=[pl.BlockSpec(m...  1.26 us

profile of v6, /device:TPU:0, one launch (start us, length us, event | category | flops | bytes accessed | tf_op | source)
XLA Modules:
  0.0 14.6 jit_solution(1985299896205750459)
XLA Ops:
  0.6 12.7 %shard_map.86 = (f32[2,32,32,128]{3,2,1,0:T(8,128)S(1)}, f32[4,64,128]{2,1,0:T(8,128)S(1)}, f32[4,32,128]{2,1,0:T(8,128)S(1)}, f32[256,128]{1,0:T(8,128)S(1)}, f...) custom-call(f32[32,32,128]{2,1,0:T(8,128)} %refs_0_.1, f32[32,32,128]{2,1,0:T(8,128)} %refs_1_.1, ...), custom_call_target="tpu_custom_call" | custom-call | tf_op jit(solution)/shard_map/pallas_call | solution.py:565
  13.3 1.3 %shard_map.87 = (f32[16,2,32,128]{3,2,1,0:T(8,128)}, f32[16,2,32,128]{3,2,1,0:T(8,128)}) custom-call(f32[2,16,2,32,128]{4,3,2,1,0:T(8,128)S(1)} %bitcast.3, f32[4,64,128]{2,1,0:T(8,128)S(1)} %get-tuple-element.11.got_edge, f32[4,32,128]{2,1,0:T(8,128)S(1)} %get-tuple-element.12.got_corner, f32[256,128]{1,0:T(8,128)S(1)} %get-tuple-element.13.level2, ...), custom_call_target="tpu_custom_call" | custom-call | tf_op jit(solution)/shard_map/pallas_call | solution.py:598

commit v7 on v6

--- a/solution.py
+++ b/solution.py
@@ -358,10 +358,11 @@
         value = dot(jnp.concatenate([high, low], 0), zh[:, at])
         return value[: high.shape[0]] + value[high.shape[0] :] + dot(high, zl[:, at])
 
-    lines2 = split(states2[16:22].reshape(192, 256))
-    lines3 = split(states3[8:15].reshape(224, 256))
-    deep2 = jnp.concatenate([deep_of(lines2, 0), jnp.zeros((64, NZ), jnp.float32)], 0)
-    deep3 = jnp.concatenate([deep_of(lines3, 1), jnp.zeros((32, NZ), jnp.float32)], 0)
+    high, low = split(jnp.concatenate([states2[16:22].reshape(192, 256), states3[8:15].reshape(224, 256)], 0))
+    value = dot(jnp.concatenate([high, low], 0), zh)
+    value = value[:416] + value[416:] + dot(high, zl)
+    deep2 = jnp.concatenate([value[:192, :128], jnp.zeros((64, NZ), jnp.float32)], 0)
+    deep3 = jnp.concatenate([value[192:, 128:], jnp.zeros((32, NZ), jnp.float32)], 0)
     both = split(jnp.concatenate([deep2, deep3], 1))
     value = times("c23", both)
     corners1 = times("c1", split(states1[...].reshape(128, 256)))

time: 14.7 us -> 14.8 us (level)
  Pallas kernels: 13.9 us -> 14.1 us
    pallas_call x1, Pallas kernels: 12.7 us -> 12.8 us  [body(): pl.pallas_call(lambda *refs: exchange(nx, ny, *refs), out_shape=passed, i...]
where the time goes in v7:
time: 14.8 us; the launch traced here: 14.7 us
  Pallas kernels  14.1 us (95%)
  between operations  0.64 us (4%)
    pallas_call x1, Pallas kernels, body(): pl.pallas_call(lambda *refs: exchange(nx, ny, *refs), out_shape=passed, i...  12.8 us
    pallas_call x1, Pallas kernels, body(): pl.pallas_call(finish, out_shape=(block, block), in_specs=[pl.BlockSpec(m...  1.26 us

profile of v7, /device:TPU:0, one launch (start us, length us, event | category | flops | bytes accessed | tf_op | source)
XLA Modules:
  0.0 14.7 jit_solution(6271271927279125609)
XLA Ops:
  0.6 12.8 %shard_map.86 = (f32[2,32,32,128]{3,2,1,0:T(8,128)S(1)}, f32[4,64,128]{2,1,0:T(8,128)S(1)}, f32[4,32,128]{2,1,0:T(8,128)S(1)}, f32[256,128]{1,0:T(8,128)S(1)}, f...) custom-call(f32[32,32,128]{2,1,0:T(8,128)} %refs_0_.1, f32[32,32,128]{2,1,0:T(8,128)} %refs_1_.1, ...), custom_call_target="tpu_custom_call" | custom-call | tf_op jit(solution)/shard_map/pallas_call | solution.py:566
  13.5 1.3 %shard_map.87 = (f32[16,2,32,128]{3,2,1,0:T(8,128)}, f32[16,2,32,128]{3,2,1,0:T(8,128)}) custom-call(f32[2,16,2,32,128]{4,3,2,1,0:T(8,128)S(1)} %bitcast.3, f32[4,64,128]{2,1,0:T(8,128)S(1)} %get-tuple-element.11.got_edge, f32[4,32,128]{2,1,0:T(8,128)S(1)} %get-tuple-element.12.got_corner, f32[256,128]{1,0:T(8,128)S(1)} %get-tuple-element.13.level2, ...), custom_call_target="tpu_custom_call" | custom-call | tf_op jit(solution)/shard_map/pallas_call | solution.py:599

commit v8 on v6

--- a/solution.py
+++ b/solution.py
@@ -461,7 +461,7 @@
         copies[3].start()
 
     for copy in sides:
-        copy.wait()
+        copy.wait_recv()
     gains = (OPS[0][3], OPS[0][4])
     both = []
     for axis in range(2):
@@ -484,7 +484,7 @@
         pl.when(jnp.logical_not(relayed[c]))(lambda: pl.semaphore_wait(relays.at[c], 1))
     for copy in edges:
         copy.wait()
-    for copy in copies:
+    for copy in copies + sides:
         copy.wait_send()
     for c in (3, 2, 1, 0):
         copies[c].wait_recv()

time: 14.7 us -> 14.7 us (level)
  no operation moved by 1% of the time
where the time goes in v8:
time: 14.7 us; the launch traced here: 14.6 us
  Pallas kernels  13.9 us (95%)
  between operations  0.64 us (4%)
    pallas_call x1, Pallas kernels, body(): pl.pallas_call(lambda *refs: exchange(nx, ny, *refs), out_shape=passed, i...  12.7 us
    pallas_call x1, Pallas kernels, body(): pl.pallas_call(finish, out_shape=(block, block), in_specs=[pl.BlockSpec(m...  1.26 us

profile of v8, /device:TPU:0, one launch (start us, length us, event | category | flops | bytes accessed | tf_op | source)
XLA Modules:
  0.0 14.6 jit_solution(13323366804269178814)
XLA Ops:
  0.6 12.7 %shard_map.86 = (f32[2,32,32,128]{3,2,1,0:T(8,128)S(1)}, f32[4,64,128]{2,1,0:T(8,128)S(1)}, f32[4,32,128]{2,1,0:T(8,128)S(1)}, f32[256,128]{1,0:T(8,128)S(1)}, f...) custom-call(f32[32,32,128]{2,1,0:T(8,128)} %refs_0_.1, f32[32,32,128]{2,1,0:T(8,128)} %refs_1_.1, ...), custom_call_target="tpu_custom_call" | custom-call | tf_op jit(solution)/shard_map/pallas_call | solution.py:565
  13.3 1.3 %shard_map.87 = (f32[16,2,32,128]{3,2,1,0:T(8,128)}, f32[16,2,32,128]{3,2,1,0:T(8,128)}) custom-call(f32[2,16,2,32,128]{4,3,2,1,0:T(8,128)S(1)} %bitcast.3, f32[4,64,128]{2,1,0:T(8,128)S(1)} %get-tuple-element.11.got_edge, f32[4,32,128]{2,1,0:T(8,128)S(1)} %get-tuple-element.12.got_corner, f32[256,128]{1,0:T(8,128)S(1)} %get-tuple-element.13.level2, ...), custom_call_target="tpu_custom_call" | custom-call | tf_op jit(solution)/shard_map/pallas_call | solution.py:598
